TPU v7x, 32 devices: a whole 2x2x4 slice. The times are simulated.
32 devices in a mesh: dp: 16 (over z, y, x), seq: 2 (over core).
Axes of the slice: x: 2, y: 2, z: 4, core: 2. Of those that a mesh axis runs over, the one named last changes fastest.
Arguments:
- dec_input: bfloat16 [48, 128, 768], P('dp'), may hold values from -6 to 6
- enc_states: bfloat16 [48, 656, 768], P('dp', 'seq'), may hold values from -6 to 6
- dec_lengths: int32 [48], P('dp'), may hold values from 32 to 128, as said below
- enc_lengths: int32 [48], P('dp'), may hold values from 358 to 656, as said below
- rel_buckets: int32 [48, 128, 128], P('dp'), may hold values from 0 to 31
- out_grad: bfloat16 [48, 128, 768], P('dp'), may hold values from -6 to 6
- gain_self: float32 [768], replicated, may hold values from 0.5 to 1.5
- gain_cross: float32 [768], replicated, may hold values from 0.5 to 1.5
- gain_ffn: float32 [768], replicated, may hold values from 0.5 to 1.5
- rel_table: float32 [32, 12], P(None, 'seq'), may hold values from -4 to 4
- self_query: bfloat16 [768, 768], P(None, 'seq'), may hold values from -0.21875 to 0.21875
- self_key: bfloat16 [768, 768], P(None, 'seq'), may hold values from -0.21875 to 0.21875
- self_value: bfloat16 [768, 768], P(None, 'seq'), may hold values from -0.21875 to 0.21875
- self_out: bfloat16 [768, 768], P('seq'), may hold values from -1 to 1
- cross_query: bfloat16 [768, 768], P(None, 'seq'), may hold values from -0.21875 to 0.21875
- cross_key: bfloat16 [768, 768], P(None, 'seq'), may hold values from -0.21875 to 0.21875
- cross_value: bfloat16 [768, 768], P(None, 'seq'), may hold values from -0.21875 to 0.21875
- cross_out: bfloat16 [768, 768], P('seq'), may hold values from -4 to 4
- ffn_in: bfloat16 [768, 3072], P(None, 'seq'), may hold values from -0.21875 to 0.21875
- ffn_out: bfloat16 [3072, 768], P('seq'), may hold values from -0.109375 to 0.109375
Outputs:
- layer_out: bfloat16 [48, 128, 768], P('dp')
- input_grad: float32 [48, 128, 768], P('dp')
- enc_grad: bfloat16 [48, 656, 768], P('dp', 'seq')
- gain_self_grad: float32 [768], replicated
- gain_cross_grad: float32 [768], replicated
- gain_ffn_grad: float32 [768], replicated
- table_grad: float32 [32, 12], P(None, 'seq')
- self_query_grad: float32 [768, 768], P(None, 'seq')
- self_key_grad: float32 [768, 768], P(None, 'seq')
- self_value_grad: float32 [768, 768], P(None, 'seq')
- self_out_grad: float32 [768, 768], P('seq')
- cross_query_grad: float32 [768, 768], P(None, 'seq')
- cross_key_grad: float32 [768, 768], P(None, 'seq')
- cross_value_grad: float32 [768, 768], P(None, 'seq')
- cross_out_grad: float32 [768, 768], P('seq')
- ffn_in_grad: float32 [768, 3072], P(None, 'seq')
- ffn_out_grad: float32 [3072, 768], P('seq')
Inputs may be any that keep to these rules, and one draw needn't show every extreme that they name: `dec_lengths`: some document has all 128 decoder tokens and some exactly 32. `enc_lengths`: each length is 656 (high resolution) or 656 * 59 // 108 (low resolution); each aligned block of 3 documents holds both.
All inputs are finite; a program needn't handle non-finite values.
Results may differ from a plain program's by a relative error of at most 0.02.
The roundings to bfloat16 on the way count: a program that leaves them out, or rounds other values in their place, can miss the bound.
Values may be sent and summed in bfloat16 or wider, within the bound.
No kernel may reach another device: no remote copies, remote signals or barrier semaphores. Data moves between devices by JAX's collectives and lax.ppermute only.
A program may use at most 192 MiB of HBM per device.

v0:
```python
import jax
import jax.numpy as jnp
from jax import lax
from jax.sharding import PartitionSpec as P

DH = 64
NB = 32


EPSILON = 1e-06
MASKED = -1e30
HIGHEST = lax.Precision.HIGHEST


def matmul(left_side, right_side):
    return jnp.einsum("btd,de->bte", left_side, right_side, preferred_element_type=jnp.float32)


def weight_grad(left_side, right_side):
    return jnp.einsum("btd,bte->de", left_side, right_side, preferred_element_type=jnp.float32)


def back_mul(grad_out, weight_array):
    return jnp.einsum("bte,de->btd", grad_out, weight_array, preferred_element_type=jnp.float32)


def rms_forward(values, scale_gain):
    inverse = lax.rsqrt(jnp.mean(values * values, axis=-1, keepdims=True) + EPSILON)
    return (values * inverse * scale_gain, inverse)


def rms_backward(values, inverse, scale_gain, grad_out):
    scaled = grad_out * scale_gain
    inner_mean = jnp.mean(scaled * values, axis=-1, keepdims=True)
    grad_in = inverse * scaled - values * inverse * inverse * inverse * inner_mean
    gain_grad = jnp.sum(grad_out * values * inverse, axis=(0, 1))
    return (grad_in, gain_grad)


def score_block(queries, key_heads, bias_term, allowed):
    scores = jnp.einsum(
        "bihd,bjhd->bhij", queries, key_heads, preferred_element_type=jnp.float32
    ) * DH ** (-0.5)
    if bias_term is not None:
        scores = scores + bias_term
    return jnp.where(allowed[:, None], scores, MASKED)


def attend_forward(queries, key_heads, values, bias_term, allowed):
    scores = score_block(queries, key_heads, bias_term, allowed)
    row_max = jnp.max(scores, axis=-1, keepdims=True)
    exp_scores = jnp.exp(scores - row_max)
    row_total = jnp.sum(exp_scores, axis=-1, keepdims=True)
    attn_probs = (exp_scores / row_total).astype(jnp.bfloat16)
    context = jnp.einsum("bhij,bjhd->bihd", attn_probs, values, preferred_element_type=jnp.float32)
    return (context.astype(jnp.bfloat16), row_max + jnp.log(row_total))


def attend_backward(queries, key_heads, values, bias_term, allowed, log_total, grad_context):
    scores = score_block(queries, key_heads, bias_term, allowed)
    attn_probs = jnp.exp(scores - log_total)
    grad_values = jnp.einsum(
        "bhij,bihd->bjhd",
        attn_probs.astype(jnp.bfloat16),
        grad_context,
        preferred_element_type=jnp.float32,
    ).astype(jnp.bfloat16)
    grad_probs = jnp.einsum(
        "bihd,bjhd->bhij", grad_context, values, preferred_element_type=jnp.float32
    )
    row_dot = jnp.sum(attn_probs * grad_probs, axis=-1, keepdims=True)
    grad_scores = (attn_probs * (grad_probs - row_dot)).astype(jnp.bfloat16)
    grad_queries = (
        jnp.einsum("bhij,bjhd->bihd", grad_scores, key_heads, preferred_element_type=jnp.float32)
        * DH ** (-0.5)
    ).astype(jnp.bfloat16)
    grad_keys = (
        jnp.einsum("bhij,bihd->bjhd", grad_scores, queries, preferred_element_type=jnp.float32)
        * DH ** (-0.5)
    ).astype(jnp.bfloat16)
    return (grad_queries, grad_keys, grad_values, grad_scores)


def shards(
    dec_input,
    enc_states,
    dec_lengths,
    enc_lengths,
    rel_buckets,
    out_grad,
    gain_self,
    gain_cross,
    gain_ffn,
    rel_table,
    self_query,
    self_key,
    self_value,
    self_out,
    cross_query,
    cross_key,
    cross_value,
    cross_out,
    ffn_in,
    ffn_out,
):
    doc_count, length = (dec_input.shape[0], dec_input.shape[1])
    enc_cols = cross_key.shape[1]

    def split_heads(tensor):
        return tensor.reshape(tensor.shape[0], tensor.shape[1], tensor.shape[2] // DH, DH)

    def merge_heads(tensor):
        return tensor.reshape(tensor.shape[0], tensor.shape[1], tensor.shape[2] * DH)

    inputs = dec_input.astype(jnp.float32)
    grads_out = out_grad.astype(jnp.float32)
    positions = jnp.arange(length, dtype=jnp.int32)
    self_allowed = (positions[None, None, :] <= positions[None, :, None]) & (
        positions[None, None, :] < dec_lengths[:, None, None]
    )
    onehot = (rel_buckets[..., None] == jnp.arange(NB, dtype=jnp.int32)).astype(jnp.float32)
    rel_bias = jnp.einsum("bijn,nh->bhij", onehot, rel_table, precision=HIGHEST)
    normed_one, inverse_one = rms_forward(inputs, gain_self)
    normed_one = normed_one.astype(jnp.bfloat16)
    self_q = split_heads(matmul(normed_one, self_query).astype(jnp.bfloat16))
    self_k = split_heads(matmul(normed_one, self_key).astype(jnp.bfloat16))
    self_v = split_heads(matmul(normed_one, self_value).astype(jnp.bfloat16))
    self_ctx, self_lse = attend_forward(self_q, self_k, self_v, rel_bias, self_allowed)
    self_ctx = merge_heads(self_ctx)
    self_branch = lax.psum(matmul(self_ctx, self_out), "seq")
    after_self = inputs + self_branch
    joined = jnp.concatenate([cross_key, cross_value], axis=1)
    full_joined = lax.all_gather(joined, "seq", axis=1, tiled=True)
    projected = matmul(enc_states, full_joined).astype(jnp.bfloat16)
    enc_kv = lax.all_to_all(projected, "seq", split_axis=2, concat_axis=1, tiled=True)
    normed_two, inverse_two = rms_forward(after_self, gain_cross)
    normed_two = normed_two.astype(jnp.bfloat16)
    cross_q = split_heads(matmul(normed_two, cross_query).astype(jnp.bfloat16))
    enc_total = enc_kv.shape[1]
    cross_k = split_heads(enc_kv[:, :, :enc_cols])
    cross_v = split_heads(enc_kv[:, :, enc_cols:])
    key_pos = jnp.arange(enc_total, dtype=jnp.int32)
    cross_allowed = jnp.broadcast_to(
        key_pos[None, None, :] < enc_lengths[:, None, None], (doc_count, length, enc_total)
    )
    cross_ctx, cross_lse = attend_forward(cross_q, cross_k, cross_v, None, cross_allowed)
    cross_ctx = merge_heads(cross_ctx)
    cross_branch = lax.psum(matmul(cross_ctx, cross_out).astype(jnp.bfloat16), "seq").astype(
        jnp.float32
    )
    after_cross = after_self + cross_branch
    normed_three, inverse_three = rms_forward(after_cross, gain_ffn)
    normed_three = normed_three.astype(jnp.bfloat16)
    hidden_pre = matmul(normed_three, ffn_in)
    activated = jax.nn.gelu(hidden_pre).astype(jnp.bfloat16)
    ffn_branch = lax.psum(matmul(activated, ffn_out).astype(jnp.bfloat16), "seq").astype(
        jnp.float32
    )
    layer_out = (after_cross + ffn_branch).astype(jnp.bfloat16)
    ffn_out_grad = weight_grad(activated, out_grad)
    grad_act = back_mul(out_grad, ffn_out)
    gelu_value, gelu_pull = jax.vjp(jax.nn.gelu, hidden_pre)
    grad_pre = gelu_pull(grad_act)[0].astype(jnp.bfloat16)
    ffn_in_grad = weight_grad(normed_three, grad_pre)
    grad_norm_three = lax.psum(back_mul(grad_pre, ffn_in).astype(jnp.bfloat16), "seq").astype(
        jnp.float32
    )
    grad_mid, gain_ffn_grad = rms_backward(after_cross, inverse_three, gain_ffn, grad_norm_three)
    grad_after_cross = grads_out + grad_mid
    grad_cross_branch = grad_after_cross.astype(jnp.bfloat16)
    cross_out_grad = weight_grad(cross_ctx, grad_cross_branch)
    grad_cross_ctx = back_mul(grad_cross_branch, cross_out).astype(jnp.bfloat16)
    cross_gq, cross_gk, cross_gv, cross_gs = attend_backward(
        cross_q, cross_k, cross_v, None, cross_allowed, cross_lse, split_heads(grad_cross_ctx)
    )
    grad_kv = jnp.concatenate([merge_heads(cross_gk), merge_heads(cross_gv)], axis=2)
    grad_kv_local = lax.all_to_all(grad_kv, "seq", split_axis=1, concat_axis=2, tiled=True)
    enc_grad = back_mul(grad_kv_local, full_joined).astype(jnp.bfloat16)
    joined_grad = lax.psum_scatter(
        weight_grad(enc_states, grad_kv_local).astype(jnp.bfloat16),
        "seq",
        scatter_dimension=1,
        tiled=True,
    ).astype(jnp.float32)
    cross_gq_merged = merge_heads(cross_gq)
    cross_key_grad = joined_grad[:, :enc_cols]
    cross_value_grad = joined_grad[:, enc_cols:]
    cross_query_grad = weight_grad(normed_two, cross_gq_merged)
    grad_norm_two = lax.psum(back_mul(cross_gq_merged, cross_query), "seq")
    grad_mid_two, gain_cross_grad = rms_backward(after_self, inverse_two, gain_cross, grad_norm_two)
    grad_after_self = grad_after_cross + grad_mid_two
    grad_self_branch = grad_after_self.astype(jnp.bfloat16)
    self_out_grad = weight_grad(self_ctx, grad_self_branch)
    grad_self_ctx = back_mul(grad_self_branch, self_out).astype(jnp.bfloat16)
    self_gq, self_gk, self_gv, self_gs = attend_backward(
        self_q, self_k, self_v, rel_bias, self_allowed, self_lse, split_heads(grad_self_ctx)
    )
    table_grad = jnp.einsum("bijn,bhij->nh", onehot, self_gs.astype(jnp.float32), precision=HIGHEST)
    self_gq_merged = merge_heads(self_gq)
    self_gk_merged = merge_heads(self_gk)
    self_gv_merged = merge_heads(self_gv)
    self_query_grad = weight_grad(normed_one, self_gq_merged)
    self_key_grad = weight_grad(normed_one, self_gk_merged)
    self_value_grad = weight_grad(normed_one, self_gv_merged)
    partial_norm = (
        back_mul(self_gq_merged, self_query)
        + back_mul(self_gk_merged, self_key)
        + back_mul(self_gv_merged, self_value)
    )
    grad_norm_one = lax.psum(partial_norm.astype(jnp.bfloat16), "seq").astype(jnp.float32)
    grad_low, gain_self_grad = rms_backward(inputs, inverse_one, gain_self, grad_norm_one)
    input_grad = grad_after_self + grad_low
    summed = lax.psum(
        (
            gain_self_grad,
            gain_cross_grad,
            gain_ffn_grad,
            table_grad,
            self_query_grad,
            self_key_grad,
            self_value_grad,
            self_out_grad,
            cross_query_grad,
            cross_key_grad,
            cross_value_grad,
            cross_out_grad,
            ffn_in_grad,
            ffn_out_grad,
        ),
        "dp",
    )
    return (
        layer_out,
        input_grad,
        enc_grad,
        summed[0],
        summed[1],
        summed[2],
        summed[3],
        summed[4],
        summed[5],
        summed[6],
        summed[7],
        summed[8],
        summed[9],
        summed[10],
        summed[11],
        summed[12],
        summed[13],
    )


def solution(mesh):
    in_specs = (
        P("dp", None, None),
        P("dp", "seq", None),
        P("dp"),
        P("dp"),
        P("dp", None, None),
        P("dp", None, None),
        P(),
        P(),
        P(),
        P(None, "seq"),
        P(None, "seq"),
        P(None, "seq"),
        P(None, "seq"),
        P("seq", None),
        P(None, "seq"),
        P(None, "seq"),
        P(None, "seq"),
        P("seq", None),
        P(None, "seq"),
        P("seq", None),
    )
    out_specs = (
        P("dp", None, None),
        P("dp", None, None),
        P("dp", "seq", None),
        P(),
        P(),
        P(),
        P(None, "seq"),
        P(None, "seq"),
        P(None, "seq"),
        P(None, "seq"),
        P("seq", None),
        P(None, "seq"),
        P(None, "seq"),
        P(None, "seq"),
        P("seq", None),
        P(None, "seq"),
        P("seq", None),
    )
    return jax.shard_map(shards, mesh=mesh, in_specs=in_specs, out_specs=out_specs, check_vma=False)
```

profile of v0, /device:TPU:0, one launch (start us, length us, event | category | flops | bytes accessed | tf_op | source)
XLA Modules:
  0.0 836.8 jit_solution(14585639054121918381)
XLA Ops:
  9.9 2.6 convolution_convert_fusion.6
  12.5 1.8 copy.148
  15.6 1.8 copy.149
  20.0 3.1 fusion.1
  23.1 2.8 copy.150
  26.1 1.9 fusion.103
  33.7 20.8 %all-reduce.10.cloned.1.call-done = f32[3,128,768]{2,1,0:T(8,128)} async-done(((f32[3,128,768]{2,1,0:T(8,128)}), f32[3,128,768]{2,1,0:T(8,128)}) %all-reduce.10.cloned.1.call-update) | async-done | bytes 1179664 | tf_op jit(solution)/shard_map/psum | solution.py:130
  54.5 1.7 multiply_reduce_fusion.5
  58.1 1.8 copy.157
  59.9 8.9 %all-gather.2.cloned.1.call-done = bf16[768,1536]{1,0:T(8,128)(2,1)} async-done(((bf16[768,768]{1,0:T(8,128)(2,1)}), bf16[768,1536]{1,0:T(8,128)(2,1)}) %all-gather.2.cloned.1.call-update) | async-done | bytes 2359312 | tf_op jit(solution)/shard_map/all_gather | solution.py:133
  68.8 6.2 fusion.4
  75.1 7.9 copy.153
  83.0 13.1 %all_to_all.36 = bf16[3,328,1536]{1,0,2:T(4,128)(2,1)} all-to-all(bf16[3,328,1536]{1,0,2:T(4,128)(2,1)} %copy.153), channel_id=1, replica_groups=mesh['dp'=16,'seq'=2] {'seq'}, dimensions={2} | all-to-all | bytes 6045696 | tf_op jit(solution)/shard_map/all_to_all | solution.py:135
  96.2 12.7 %copy.208 = bf16[3,328,2,768]{3,2,1,0:T(2,128)(2,1)} copy(bf16[3,328,2,768]{1,0,3,2:T(4,128)(2,1)} %bitcast.171) | data formatting | bytes 6045696 | tf_op jit(solution)/shard_map/all_to_all | solution.py:135
  108.8 2.2 copy.155
  111.1 1.9 fusion.101
  113.0 3.8 copy.158
  116.7 3.8 copy.156
  120.5 3.2 fusion.104
  124.6 1.8 copy-done.2
  129.4 20.1 %all-reduce.12.cloned.1.call-done = bf16[3,128,768]{2,1,0:T(8,128)(2,1)} async-done(((bf16[3,128,768]{2,1,0:T(8,128)(2,1)}), bf16[3,128,768]{2,1,0:T(8,128)(2,1)}) %all-reduce.12.cloned.1.call-update) | async-done | bytes 589840 | tf_op jit(solution)/shard_map/psum | solution.py:148
  153.6 2.2 fusion.18
  156.8 1.9 fusion.45
  159.7 19.2 %all-reduce.14.cloned.1.call-done = bf16[3,128,768]{2,1,0:T(8,128)(2,1)} async-done(((bf16[3,128,768]{2,1,0:T(8,128)(2,1)}), bf16[3,128,768]{2,1,0:T(8,128)(2,1)}) %all-reduce.14.cloned.1.call-update) | async-done | bytes 589840 | tf_op jit(solution)/shard_map/psum | solution.py:165
  178.9 2.2 fusion.65
  183.4 5.5 fusion.32
  188.9 4.5 multiply_reduce_fusion
  196.0 2.5 multiply_convert_fusion.1
  198.5 5.0 copy.170
  203.6 5.1 copy.169
  210.3 4.0 pad_maximum_fusion
  214.3 7.1 all_to_all.37
  223.7 4.0 fusion.11
  229.0 4.5 convolution_bitcast_fusion.1
  233.5 3.8 convolution_bitcast_fusion
  237.3 2.3 fusion.48
  241.3 2.3 multiply_reduce_fusion.1
  246.2 1.8 copy.162
  265.1 2.9 fusion.102
  268.0 6.3 fusion.35
  275.6 2.9 fusion.70
  278.5 2.2 fusion.69
  280.8 80.8 %all-reduce = (f32[768]{0:T(1024)}, f32[768]{0:T(1024)}, f32[768]{0:T(1024)}, f32[32,6]{0,1:T(8,128)}) all-reduce(f32[768]{0:T(1024)} %get-tuple-element.89, f32[768]{0:T(1024)S(1)} %copy-done.81, f32[768]{0:T(1024)S(1)} %copy-done.80, f32[32,6]{0,1:T(8,128)} %fusion.70), channel_id=1, replica_groups=mesh['dp'=16,'seq'=2] {'dp'}, use_global_device_ids=true, to_apply=%region_19.20 | all-reduce | flops 2496 | bytes 19968 | tf_op jit(solution)/shard_map/psum | solution.py:213
  362.3 2.7 fusion.60
  365.0 442.0 %all-reduce.18.cloned.1.call-done = (f32[768,384]{1,0:T(8,128)}, f32[768,384]{1,0:T(8,128)}, f32[768,384]{1,0:T(8,128)}, f32[384,768]{1,0:T(8,128)}, f32[768,384...) async-done(((f32[768,384]{1,0:T(8,128)}, f32[768,384]{1,0:T(8,128)}, ...) | async-done | bytes 18874384 | tf_op jit(solution)/shard_map/psum | solution.py:213
  807.0 2.7 copy.184
  820.6 5.5 copy.232
  826.2 2.4 copy.233
  (260 shorter events, 68.7 us)
Async XLA Ops:
  7.2 144.5 %copy-start = (bf16[768,1536]{1,0:T(8,128)(2,1)S(1)}, bf16[768,1536]{1,0:T(8,128)(2,1)}, u32[]{:S(2)}) copy-start(bf16[768,1536]{1,0:T(8,128)(2,1)} %param.38) | copy-start | bytes 7077892
  7.2 47.3 %all-reduce.10.cloned.1.call-start = ((), (), s32[]{:S(2)}) async-start(), calls=%async_computation.3 | async-start | bytes 2359296 | tf_op jit(solution)/shard_map/psum | solution.py:130
  9.9 7.6 copy-start.70
  9.9 4.5 copy-start.7
  9.9 4.5 copy-start.57
  9.9 4.4 copy-start.68
  17.5 2.5 copy-start.64
  17.5 2.5 copy-start.82
  23.1 2.8 copy-start.74
  31.8 37.0 %all-gather.2.cloned.1.call-start = ((), (), s32[]{:S(2)}) async-start(), calls=%async_computation.4 | async-start | bytes 3538944 | tf_op jit(solution)/shard_map/all_gather | solution.py:133
  33.0 116.5 %all-reduce.12.cloned.1.call-start = ((), (), s32[]{:S(2)}) async-start(), calls=%async_computation.5 | async-start | bytes 1179648 | tf_op jit(solution)/shard_map/psum | solution.py:148
  33.7 23.1 %copy-start.72 = (f32[768]{0:T(1024)S(1)}, f32[768]{0:T(1024)}, u32[]{:S(2)}) copy-start(f32[768]{0:T(1024)} %param.27) | copy-start | bytes 9220
  54.5 2.4 copy-start.35
  56.2 18.9 %copy-start.3 = (f32[3,128,768]{2,1,0:T(8,128)}, f32[3,128,768]{2,1,0:T(8,128)S(1)}, u32[]{:S(2)}) copy-start(f32[3,128,768]{2,1,0:T(8,128)S(1)} %get-tuple-element.110) | copy-start | bytes 3538948
  116.7 3.8 copy-start.18
  123.7 2.7 copy-start.2
  123.8 2.7 copy-start.67
  123.8 2.8 copy-start.12
  124.6 3.4 copy-start.79
  129.3 22.4 %copy-start.63 = (f32[768]{0:T(1024)S(1)}, f32[768]{0:T(1024)}, u32[]{:S(2)}) copy-start(f32[768]{0:T(1024)} %param.28) | copy-start | bytes 9220
  129.3 49.6 %all-reduce.14.cloned.1.call-start = ((), (), s32[]{:S(2)}) async-start(), calls=%async_computation.6 | async-start | bytes 1179648 | tf_op jit(solution)/shard_map/psum | solution.py:165
  158.8 82.5 %all-reduce.16.cloned.1.call-start = ((), (), s32[]{:S(2)}) async-start(), calls=%async_computation.7 | async-start | bytes 2359296 | tf_op jit(solution)/shard_map/psum | solution.py:189
  183.4 5.6 copy-start.13
  183.4 10.1 %slice-start = ((s8[6045696]{0:T(1024)(128)(4,1)}), s8[4194304]{0:T(1024)(128)(4,1)S(1)}, s32[]{:S(2)}) async-start(s8[6045696]{0:T(1024)(128)(4,1)} %bitcast.169), calls=%async_computation.11 | async-start | bytes 8388608
  188.9 4.6 slice-start.1
  196.0 12.7 %copy-start.20 = (bf16[3,6,64,128]{3,2,1,0:T(8,128)(2,1)}, bf16[3,6,64,128]{3,2,1,0:T(8,128)(2,1)S(1)}, u32[]{:S(2)}) copy-start(bf16[3,6,64,128]{3,2,1,0:T(8,128)(2,1)S(1)} %fusion.54) | copy-start | bytes 884740
  203.5 5.1 copy-start.36
  210.2 54.9 %reduce-scatter.2.cloned.1.call-start = ((), (), s32[]{:S(2)}) async-start(), calls=%async_computation.8 | async-start | bytes 3538944 | tf_op jit(solution)/shard_map/reduce_scatter | solution.py:179
  227.7 50.8 %all-reduce.20.cloned.1.call-start = ((), (), s32[]{:S(2)}) async-start(), calls=%async_computation.10 | async-start | bytes 2359296 | tf_op jit(solution)/shard_map/psum | solution.py:156
  229.0 4.5 copy-start.34
  229.0 4.5 copy-start.56
  233.5 3.8 copy-start.85
  237.3 2.3 copy-start.21
  237.3 2.3 copy-start.73
  245.0 3.1 copy-start.6
  256.2 2.4 copy-start.8
  256.2 2.4 copy-start.30
  256.2 2.4 copy-start.69
  256.2 2.4 copy-start.71
  256.2 550.7 %all-reduce.18.cloned.1.call-start = ((), (), s32[]{:S(2)}) async-start(), calls=%async_computation.9 | async-start | bytes 37748736 | tf_op jit(solution)/shard_map/psum | solution.py:213
  268.0 6.3 copy-start.15
  275.6 5.2 copy-start.80
  275.6 5.2 copy-start.81
  278.5 83.7 %copy-start.31 = (bf16[3,128,768]{2,1,0:T(8,128)(2,1)S(1)}, bf16[3,128,768]{2,1,0:T(8,128)(2,1)}, u32[]{:S(2)}) copy-start(bf16[3,128,768]{2,1,0:T(8,128)(2,1)} %get-tuple-element.106) | copy-start | bytes 1769476
  807.0 2.8 copy-start.50
  819.6 6.5 slice-start.2
  820.6 5.5 slice-start.3
  826.2 3.4 copy-start.1
  (51 other events, 76.3 us)
Sparse Core Ops, SparseCore 0:
  31.9 22.5 all-reduce.9
  56.7 12.1 all-gather.1
  129.4 19.9 all-reduce.11
  158.9 20.0 all-reduce.13
  210.3 20.9 all-reduce.15
  233.5 11.0 reduce-scatter.1
  256.3 21.0 all-reduce.19
  285.5 521.4 all-reduce.17
where the time goes:
time: 846 us; the launch traced here: 837 us
  waiting for transfers between devices  511 us (60%)
  blocking collectives  101 us (12%)
  local copies, waits for them, and re-layouts  94.9 us (11%)
  matrix products  86 us (10%)
  other arithmetic  27.5 us (3%)
  between operations  15.3 us (2%)
    psum x1, waiting for transfers between devices, shards(): lax.psum((gain_self_grad, gain_cross_grad, gain_ffn_grad, table_grad, sel...  442 us
    psum x1, blocking collectives, shards(): lax.psum((gain_self_grad, gain_cross_grad, gain_ffn_grad, table_grad, sel...  80.8 us
    unnamed x192, local copies, waits for them, and re-layouts  36.4 us
    dot_general x9, matrix products, weight_grad(): jnp.einsum('btd,bte->de', left_side, right_side, preferred_element_type=j...  21.8 us
    psum x1, waiting for transfers between devices, shards(): self_branch = lax.psum(matmul(self_ctx, self_out), 'seq')  20.8 us
    psum x1, waiting for transfers between devices, shards(): lax.psum(matmul(cross_ctx, cross_out).astype(jnp.bfloat16), 'seq')  20.1 us
    psum x1, waiting for transfers between devices, shards(): lax.psum(back_mul(grad_pre, ffn_in).astype(jnp.bfloat16), 'seq')  19.2 us
    dot_general x9, matrix products, matmul(): jnp.einsum('btd,de->bte', left_side, right_side, preferred_element_type=j...  19.2 us
  transfers between devices with their start and end apart: 8, of which 5 were waited for; matrix products, arithmetic and copies ran while one was open for 8% of the time, Pallas kernels for 0%

commit v1 on v0

v1 whole, which is shorter than its diff:
```python
import functools

import jax
import jax.numpy as jnp
from jax import lax
from jax.experimental import pallas as pl
from jax.experimental.pallas import tpu as pltpu
from jax.sharding import PartitionSpec as P

DH = 64
NB = 32
PAIR = 2 * DH
SCALE = DH**-0.5
EPSILON = 1e-06
MASKED = -1e30
F32 = jnp.float32
BF16 = jnp.bfloat16
MIB = 1024 * 1024
SUM_LIMIT = 16


def dot(a, b):
    return lax.dot_general(a, b, (((1,), (0,)), ((), ())), preferred_element_type=F32)


def dot_nt(a, b):
    return lax.dot_general(a, b, (((1,), (1,)), ((), ())), preferred_element_type=F32)


def dot_tn(a, b):
    return lax.dot_general(a, b, (((0,), (0,)), ((), ())), preferred_element_type=F32)


VMEM = pl.BlockSpec(memory_space=pltpu.VMEM)
SMEM = pl.BlockSpec(memory_space=pltpu.SMEM)
ANY = pl.BlockSpec(memory_space=pl.ANY)


def kernel(body, name, outs, ins, after=(), smem=0, in_specs=None, out_specs=None, scratch=(), grid=None, limit=30, aliases=None, us=0.5):
    n_in, n_after = len(ins), len(after)

    def wrapped(*refs):
        body(*refs[:n_in], *refs[n_in + n_after :])

    in_specs = list(in_specs) if in_specs is not None else [VMEM] * (n_in - smem)
    out_specs = list(out_specs) if out_specs is not None else [VMEM] * len(outs)
    params = pltpu.CompilerParams(vmem_limit_bytes=limit * MIB)
    cost = pl.CostEstimate(flops=int(us * 10e9), bytes_accessed=0, transcendentals=0)
    shapes = [jax.ShapeDtypeStruct(s, t) for s, t in outs]
    if grid is None:
        call = pl.pallas_call(
            wrapped,
            name=name,
            out_shape=shapes,
            in_specs=[SMEM] * smem + in_specs + [ANY] * n_after,
            out_specs=out_specs,
            scratch_shapes=list(scratch),
            compiler_params=params,
            cost_estimate=cost,
            input_output_aliases=aliases or {},
        )
    else:
        call = pl.pallas_call(
            wrapped,
            name=name,
            out_shape=shapes,
            grid_spec=pltpu.PrefetchScalarGridSpec(
                num_scalar_prefetch=smem,
                grid=grid,
                in_specs=in_specs + [ANY] * n_after,
                out_specs=out_specs,
                scratch_shapes=list(scratch),
            ),
            compiler_params=params,
            cost_estimate=cost,
            input_output_aliases=aliases or {},
        )
    return call(*ins, *after)


def pin(*arrays):
    return [pltpu.with_memory_space_constraint(a, pltpu.HBM) for a in arrays]


def whole(shape):
    return pl.BlockSpec(shape, lambda *_: (0,) * len(shape))


def step_block(shape, axis=0):
    return pl.BlockSpec(shape, lambda i, *_: tuple(i if a == axis else 0 for a in range(len(shape))))


def inverse_rms(values):
    return lax.rsqrt(jnp.mean(values * values, axis=-1, keepdims=True) + EPSILON)


def row_of(gain):
    return gain[...].reshape(1, gain.shape[0])


def rms_backward(values, gain, grad):
    inverse = inverse_rms(values)
    scaled = grad * gain
    inner = jnp.mean(scaled * values, axis=-1, keepdims=True)
    grad_in = inverse * scaled - values * (inverse * inverse * inverse * inner)
    return grad_in, jnp.sum(grad * values * inverse, axis=0, keepdims=True)


def stack_pair(pair, scale=1.0):
    lanes = lax.broadcasted_iota(jnp.int32, (1, PAIR), 1)
    low = jnp.where(lanes < DH, scale, 0.0).astype(BF16)
    high = jnp.where(lanes < DH, 0.0, scale).astype(BF16)
    return jnp.concatenate([pair * low, pair * high], axis=0)


def join_pair(turned):
    n = turned.shape[1] // 2
    return jnp.concatenate([turned[:DH, :n], turned[DH:, n:]], axis=0).T


def fold(op, parts):
    return functools.reduce(op, parts)


def attend(q2, keys, values, biases):
    scores = [dot_nt(k, q2) + b for k, b in zip(keys, biases)]
    top = fold(jnp.maximum, [jnp.max(s, axis=0, keepdims=True) for s in scores])
    exps = [jnp.exp(s - top) for s in scores]
    total = fold(jnp.add, [jnp.sum(e, axis=0, keepdims=True) for e in exps])
    inv = 1.0 / total
    out = fold(jnp.add, [dot_tn(v, (e * inv).astype(BF16)) for e, v in zip(exps, values)])
    return out, top + jnp.log(total)


def attend_back(q2, do2, lse, keys, values, biases):
    probs = [jnp.exp(dot_nt(k, q2) + b - lse) for k, b in zip(keys, biases)]
    dv = [dot(p.astype(BF16), do2).astype(BF16) for p in probs]
    dp = [dot_nt(v, do2) for v in values]
    row = fold(jnp.add, [jnp.sum(p * g, axis=0, keepdims=True) for p, g in zip(probs, dp)])
    ds = [(p * (g - row)).astype(BF16) for p, g in zip(probs, dp)]
    dq = fold(jnp.add, [dot_tn(k, s) for s, k in zip(ds, keys)])
    dk = [dot(s, q2).astype(BF16) for s in ds]
    return dq, ds, dk, dv


def twice(a):
    return jnp.concatenate([a, a], axis=1)


def self_hidden(length, size):
    keys = lax.broadcasted_iota(jnp.int32, (size, size), 0)
    queries = lax.broadcasted_iota(jnp.int32, (size, size), 1)
    return jnp.where((keys <= queries) & (keys < length), 0.0, MASKED)


def cross_hidden(length, core, size, half):
    out = []
    for part in (core, 1 - core):
        pos = lax.broadcasted_iota(jnp.int32, (half, size), 0) + part * half
        out.append(twice(jnp.where(pos < length, 0.0, MASKED)))
    return out


def table_lines(table):
    lanes = lax.broadcasted_iota(jnp.int32, (1, 128), 1)
    lines = []
    for head in range(table.shape[0]):
        line = jnp.zeros((1, 128), F32)
        for b in range(NB):
            line = jnp.where(lanes == b, table[head, b], line)
        lines.append(line)
    return lines


def pair_bias(lines, index, pair, hidden):
    cols = []
    for head in (2 * pair, 2 * pair + 1):
        line = jnp.broadcast_to(lines[head], index.shape)
        cols.append(jnp.take_along_axis(line, index, axis=1, mode="promise_in_bounds") + hidden)
    return jnp.concatenate(cols, axis=1)


def self_forward(lens, table, x, gain, wq, wk, wv, buckets, h_o, q_o, k_o, v_o, o_o, lse_o):
    docs, size = buckets.shape[0], buckets.shape[1]
    xf = x[...].astype(F32)
    h = (xf * inverse_rms(xf) * row_of(gain)).astype(BF16)
    h_o[...] = h
    q_o[...] = dot(h, wq[...]).astype(BF16)
    k_o[...] = dot(h, wk[...]).astype(BF16)
    v_o[...] = dot(h, wv[...]).astype(BF16)
    lines = table_lines(table)
    pairs = wq.shape[1] // PAIR
    for d in range(docs):
        rows = slice(d * size, (d + 1) * size)
        hidden = self_hidden(lens[d], size)
        index = buckets[d].T
        for p in range(pairs):
            cols = slice(p * PAIR, (p + 1) * PAIR)
            q2 = stack_pair(q_o[rows, cols], SCALE)
            bias = pair_bias(lines, index, p, hidden)
            out, lse = attend(q2, [k_o[rows, cols]], [v_o[rows, cols]], [bias])
            o_o[rows, cols] = join_pair(out).astype(BF16)
            at = d * pairs + p
            lse_o[at : at + 1, :] = lse


def project_kv(e, wk, wv, kv_o):
    n = wk.shape[1]
    kv_o[0, :, :n] = dot(e[0], wk[...]).astype(BF16)
    kv_o[0, :, n:] = dot(e[0], wv[...]).astype(BF16)


def cross_forward(meta, lens, x, o_own, o_oth, wo_own, wo_oth, gain, wq, kv_own, kv_oth, x1_o, h_o, q_o, o_o, lse_o):
    half, n = kv_own.shape[1], wq.shape[1]
    size = o_o.shape[0]
    doc = pl.program_id(0)

    @pl.when(doc == 0)
    def _():
        x1 = x[...].astype(F32) + (dot(o_own[...], wo_own[...]) + dot(o_oth[...], wo_oth[...]))
        x1_o[...] = x1
        h = (x1 * inverse_rms(x1) * row_of(gain)).astype(BF16)
        h_o[...] = h
        q_o[...] = dot(h, wq[...]).astype(BF16)

    hidden = cross_hidden(lens[doc], meta[2], size, half)
    q = q_o[pl.ds(pl.multiple_of(doc * size, size), size), :]
    for p in range(n // PAIR):
        cols = slice(p * PAIR, (p + 1) * PAIR)
        vals = slice(n + p * PAIR, n + (p + 1) * PAIR)
        out, lse = attend(
            stack_pair(q[:, cols], SCALE),
            [kv_own[0, :, cols], kv_oth[0, :, cols]],
            [kv_own[0, :, vals], kv_oth[0, :, vals]],
            hidden,
        )
        o_o[:, cols] = join_pair(out).astype(BF16)
        lse_o[0, p : p + 1, :] = lse


GELU_C = 0.7978845608028654
GELU_A = 0.044715


def grid_slot(i):
    return jnp.where(i < 2, 2 * i + 1, 2 * (i - 2))


def ffn_act_grad(meta, dy, wout, dz_o):
    dz_o[0] = dot_nt(dy[...], wout[...])


def ffn_forward(meta, x1, o_own, o_oth, wo_own, wo_oth, gain, win, dz, x2_o, z_send, z_keep, du_send, du_keep, part_o, h_s, total):
    i = pl.program_id(0)

    @pl.when(i == 0)
    def _():
        x2 = x1[...] + (dot(o_own[...], wo_own[...]) + dot(o_oth[...], wo_oth[...]))
        x2_o[...] = x2
        h = (x2 * inverse_rms(x2) * row_of(gain)).astype(BF16)
        h_s[...] = h
        half = h.shape[1] // 2
        du_send[2] = h[:, :half]
        du_send[3] = h[:, half:]

    u = dot(h_s[...], win[...])
    u2 = u * u
    t = jnp.tanh(GELU_C * (u + GELU_A * (u * u2)))
    g = 0.5 * (1.0 + t)
    slope = g + (0.5 * GELU_C) * u * (1.0 - t * t) * (1.0 + 3.0 * GELU_A * u2)
    z = (u * g).astype(BF16)
    du = (dz[0] * slope).astype(BF16)
    z_slot = meta[0] ^ grid_slot(i) ^ meta[3]

    @pl.when((z_slot & 1) == 1)
    def _():
        z_send[z_slot >> 1] = z

    @pl.when((z_slot & 1) == 0)
    def _():
        z_keep[z_slot >> 1] = z

    @pl.when(i < 2)
    def _():
        du_send[i] = du

    @pl.when(i >= 2)
    def _():
        du_keep[i - 2] = du

    grad = dot_nt(du, win[...])

    @pl.when(i == 0)
    def _():
        total[...] = grad

    @pl.when((i > 0) & (i < 3))
    def _():
        total[...] += grad

    @pl.when(i == 3)
    def _():
        part_o[...] = (total[...] + grad).astype(BF16)


def ffn_out_grads(meta, keep, got, dy, dy_got, keep_o, send_o):
    half = dy.shape[1] // 2
    for j, out in enumerate((keep_o, send_o)):
        w = (dot_tn(keep[j], dy[...]) + dot_tn(got[j], dy_got[...])).astype(BF16)
        r = w.shape[0] // 4
        for az in range(4):
            for k in range(2):
                out[meta[1] ^ az, k * r : (k + 1) * r] = w[az * r : (az + 1) * r, k * half : (k + 1) * half]


def ffn_in_grads(meta, keep, send, got, keep_o, send_o):
    for j, out in enumerate((keep_o, send_o)):
        for k in range(2):
            w = (dot_tn(send[2 + k], keep[j]) + dot_tn(got[2 + k], got[j])).astype(BF16)
            r = w.shape[0] // 2
            for az in range(2):
                out[meta[1] ^ (2 * k + az)] = w[az * r : (az + 1) * r]


def ffn_branch(meta, send, keep, wout, part_o, total):
    i = pl.program_id(0)
    branch = dot(jnp.where(i < 2, send[0], keep[0]), wout[...])

    @pl.when(i == 0)
    def _():
        total[...] = branch

    @pl.when((i > 0) & (i < 3))
    def _():
        total[...] += branch

    @pl.when(i == 3)
    def _():
        part_o[...] = (total[...] + branch).astype(BF16)


def finish_output(x2, p_own, p_oth, y_o):
    y_o[...] = (x2[...] + (p_own[...].astype(F32) + p_oth[...].astype(F32))).astype(BF16)


def cross_backward(meta, lens, x2, p_own, p_oth, gain, dy, wo, q, lse, kv_own, kv_oth, gain_o, dx2_o, dc_o, dq_o, dkv_own, dkv_oth, do_s):
    half, n = kv_own.shape[1], q.shape[1]
    size = q.shape[0]
    doc = pl.program_id(0)

    @pl.when(doc == 0)
    def _():
        dv, gain_grad = rms_backward(x2[...], row_of(gain), p_own[...].astype(F32) + p_oth[...].astype(F32))
        gain_o[...] = gain_grad
        dx2 = dy[...].astype(F32) + dv
        dx2_o[...] = dx2
        dc = dx2.astype(BF16)
        dc_o[...] = dc
        do_s[...] = dot_nt(dc, wo[...]).astype(BF16)

    hidden = cross_hidden(lens[doc], meta[2], size, half)
    do = do_s[pl.ds(pl.multiple_of(doc * size, size), size), :]
    for p in range(n // PAIR):
        cols = slice(p * PAIR, (p + 1) * PAIR)
        vals = slice(n + p * PAIR, n + (p + 1) * PAIR)
        dq, _, dk, dv = attend_back(
            stack_pair(q[:, cols], SCALE),
            stack_pair(do[:, cols]),
            lse[0, p : p + 1, :],
            [kv_own[0, :, cols], kv_oth[0, :, cols]],
            [kv_own[0, :, vals], kv_oth[0, :, vals]],
            hidden,
        )
        dq_o[:, cols] = (join_pair(dq) * SCALE).astype(BF16)
        dkv_own[0, :, cols], dkv_oth[0, :, cols] = dk
        dkv_own[0, :, vals], dkv_oth[0, :, vals] = dv


def store_tensors(tensors, zq, scratch):
    for t, quarters in enumerate(tensors):
        for az, quarter in enumerate(quarters):
            scratch[t, zq ^ az] = quarter.astype(BF16)


def tall(a):
    r = a.shape[0] // 4
    return [a[z * r : (z + 1) * r] for z in range(4)]


def wide(a):
    r, c = a.shape[0] // 2, a.shape[1] // 2
    return [a[(z % 2) * r : (z % 2 + 1) * r, (z // 2) * c : (z // 2 + 1) * c] for z in range(4)]


def send_blocks(quad, scratch, keep, send, sem):
    copies = []
    for s in range(4):
        ref = keep if s % 2 == 0 else send
        copies.append(pltpu.make_async_copy(scratch.at[quad ^ s], ref.at[s // 2], sem.at[s]))
    for c in copies:
        c.start()
    for c in copies:
        c.wait()


def cross_grads(meta, h, dq, e_own, e_oth, dkv_own, dkv_oth, dc, o, keep, send, scratch, sem):
    n = dq.shape[1]
    kv = dot_tn(e_own[...], dkv_own[...]) + dot_tn(e_oth[...], dkv_oth[...])
    gq = dot_tn(h[...], dq[...])
    go = dot_tn(o[...], dc[...])
    store_tensors([tall(gq), tall(kv[:, :n]), tall(kv[:, n:]), wide(go)], meta[1], scratch)
    send_blocks(meta[0], scratch, keep, send, sem)


def self_backward(lens, table, x1, dx2, dq_own, dq_oth, wq_own, wq_oth, gain, wo, q, k, v, lse, buckets, gain_o, dx1_o, da_o, dqkv_o, ds_o):
    docs, size = buckets.shape[0], buckets.shape[1]
    n = q.shape[1]
    dh = dot_nt(dq_own[...], wq_own[...]) + dot_nt(dq_oth[...], wq_oth[...])
    dv, gain_grad = rms_backward(x1[...], row_of(gain), dh)
    gain_o[...] = gain_grad
    dx1 = dx2[...] + dv
    dx1_o[...] = dx1
    da = dx1.astype(BF16)
    da_o[...] = da
    do = dot_nt(da, wo[...]).astype(BF16)
    lines = table_lines(table)
    pairs = n // PAIR
    for d in range(docs):
        rows = slice(d * size, (d + 1) * size)
        hidden = self_hidden(lens[d], size)
        index = buckets[d].T
        for p in range(pairs):
            cols = slice(p * PAIR, (p + 1) * PAIR)
            at = d * pairs + p
            dq, ds, dk, dvv = attend_back(
                stack_pair(q[rows, cols], SCALE),
                stack_pair(do[rows, cols]),
                lse[at : at + 1, :],
                [k[rows, cols]],
                [v[rows, cols]],
                [pair_bias(lines, index, p, hidden)],
            )
            dqkv_o[rows, cols] = (join_pair(dq) * SCALE).astype(BF16)
            dqkv_o[rows, n + p * PAIR : n + (p + 1) * PAIR] = dk[0]
            dqkv_o[rows, 2 * n + p * PAIR : 2 * n + (p + 1) * PAIR] = dvv[0]
            ds_o[p, d] = ds[0]


def self_input(dqkv, wq, wk, wv, part_o):
    n = wq.shape[1]
    part_o[...] = (
        dot_nt(dqkv[:, :n], wq[...])
        + dot_nt(dqkv[:, n : 2 * n], wk[...])
        + dot_nt(dqkv[:, 2 * n :], wv[...])
    ).astype(BF16)


def self_grads(meta, h, dqkv, da, o, keep, send, scratch, sem):
    n = o.shape[1]
    g = dot_tn(h[...], dqkv[...])
    go = dot_tn(o[...], da[...])
    store_tensors([tall(g[:, t * n : (t + 1) * n]) for t in range(3)] + [wide(go)], meta[1], scratch)
    send_blocks(meta[0], scratch, keep, send, sem)


def finish_input(x, p_own, p_oth, gain, dx1, gain_o, dx_o):
    dv, gain_grad = rms_backward(
        x[...].astype(F32), row_of(gain), p_own[...].astype(F32) + p_oth[...].astype(F32)
    )
    gain_o[...] = gain_grad
    dx_o[...] = dx1[...] + dv


def small_grads(buckets, ds, gain1, gain2, gain3, out):
    docs, size = buckets.shape[0], buckets.shape[1]
    pairs = ds.shape[0]
    half = out.shape[1]
    lanes = lax.broadcasted_iota(jnp.int32, (8, 128), 1)
    subs = lax.broadcasted_iota(jnp.int32, (8, 128), 0)
    out[...] = jnp.zeros(out.shape, F32)
    for j, gain in enumerate((gain1, gain2, gain3)):
        for k in range(2):
            out[2 * j + k : 2 * j + k + 1, :] = gain[:, k * half : (k + 1) * half]
    table = jnp.zeros((8, 128), F32)
    index = [twice(buckets[d].T) for d in range(docs)]
    for p in range(pairs):
        for b in range(NB):
            line = fold(
                jnp.add,
                [
                    jnp.sum(jnp.where(index[d] == b, ds[p, d].astype(F32), 0.0), axis=0, keepdims=True)
                    for d in range(docs)
                ],
            )
            for j in range(2):
                total = jnp.sum(line[:, j * size : (j + 1) * size], axis=1, keepdims=True)
                table = jnp.where((subs == 2 * p + j) & (lanes == b), total, table)
    out[8:16, :128] = table


def enc_part(dkv, wk, wv, out):
    n = wk.shape[1]
    out[0] = (dot_nt(dkv[0, :, :n], wk[...]) + dot_nt(dkv[0, :, n:], wv[...])).astype(BF16)


def finish_enc(dkv, wk, wv, got, out):
    n = wk.shape[1]
    own = dot_nt(dkv[0, :, :n], wk[...]) + dot_nt(dkv[0, :, n:], wv[...])
    out[0] = (own + got[0].astype(F32)).astype(BF16)


def add_quads(keep, got, keep_o, send_o):
    keep_o[...] = keep[0] + got[0]
    send_o[...] = keep[1] + got[1]


EXTRA = 16


def add_quads(keep, got, keep_o, send_o):
    keep_o[...] = keep[0] + got[0]
    send_o[...] = keep[1] + got[1]


def add_pieces(keep, got, keep_o, send_o):
    for j in range(2):
        keep_o[j] = keep[2 * j] + got[2 * j]
        send_o[j] = keep[2 * j + 1] + got[2 * j + 1]


def add_pair(keep, got, keep_o, send_o):
    keep_o[...] = keep[0] + got[0]
    send_o[...] = keep[1] + got[1]


def add_shard(keep, got, out):
    out[...] = keep[...] + got[...]


def put_two(a, b, out):
    out[0] = a[...]
    out[1] = b[...]


def join_pieces(meta, own, got, out):
    r = own.shape[1]
    for j in range(2):
        out[pl.ds(pl.multiple_of((meta[1] ^ (2 * j)) * r, r), r), :] = own[j]
        out[pl.ds(pl.multiple_of((meta[1] ^ (2 * j + 1)) * r, r), r), :] = got[j]


def put_blocks(a, b, out):
    r = a.shape[0]
    out[:r] = a[...]
    out[r:] = b[...]


def plus_small(own, got):
    return (own[...].astype(BF16).astype(F32) + got.astype(F32)).astype(BF16)


def self_quads(keep, got, small, keep_o, send_o):
    keep_o[...] = keep[0] + got[0]
    r = keep.shape[2]
    for z in range(4):
        send_o[z * r : (z + 1) * r] = keep[1, z] + got[1, z]
    send_o[4 * r :] = small[...].astype(BF16)


def self_pieces(keep, got, small, keep_o, send_o, small_o):
    r = keep.shape[1]
    total = plus_small(small, got[4 * r :])
    small_o[...] = total
    for j in range(2):
        keep_o[j] = keep[2 * j] + got[2 * j * r : (2 * j + 1) * r]
        send_o[j * r : (j + 1) * r] = keep[2 * j + 1] + got[(2 * j + 1) * r : (2 * j + 2) * r]
    send_o[2 * r :] = total


def self_pair(keep, got, small, keep_o, send_o, small_o):
    r = keep.shape[1]
    total = plus_small(small, got[2 * r :])
    small_o[...] = total
    keep_o[...] = keep[0] + got[:r]
    send_o[:r] = keep[1] + got[r : 2 * r]
    send_o[r:] = total


def self_shard(keep, got, small, out, small_o):
    r = keep.shape[0]
    out[...] = keep[...] + got[:r]
    small_o[...] = plus_small(small, got[r:])


def self_blocks(a, b, small, out):
    r = a.shape[0]
    out[:r] = a[...]
    out[r : 2 * r] = b[...]
    out[2 * r :] = small[...]


def write_small(own, got, gain1_o, gain2_o, gain3_o, table_o):
    total = own[...].astype(F32) + got[got.shape[0] - EXTRA :, :].astype(F32)
    for j, gain in enumerate((gain1_o, gain2_o, gain3_o)):
        gain[...] = jnp.concatenate([total[2 * j : 2 * j + 1], total[2 * j + 1 : 2 * j + 2]], axis=1).reshape(gain.shape)
    heads, buckets = table_o.shape
    table_o[...] = total[8 : 8 + heads, :buckets]


def write_ffn_out(slots, meta, both, *refs):
    out, done, scratch, sem = refs[-4:]
    done[...] = jnp.zeros(done.shape, F32)
    r, c = scratch.shape[1] // 4, scratch.shape[2] // 2
    copies = []
    for i, s in enumerate(slots):
        for z in range(4):
            for j in range(2):
                at = (8 * i + 2 * z + j) * r
                scratch[i, z * r : (z + 1) * r, j * c : (j + 1) * c] = both[at : at + r].astype(F32)
        copies.append(pltpu.make_async_copy(scratch.at[i], out.at[meta[0] ^ s], sem.at[i]))
        copies[-1].start()
    for copy in copies:
        copy.wait()


def write_ffn_in(slots, meta, both, *refs):
    out, done, scratch, sem = refs[-4:]
    done[...] = jnp.zeros(done.shape, F32)
    r, c = scratch.shape[1:]
    copies = []
    for i, s in enumerate(slots):
        scratch[i] = both[i * r : (i + 1) * r].astype(F32)
        cols = pl.ds(pl.multiple_of((meta[0] ^ s) * c, 128), c)
        copies.append(pltpu.make_async_copy(scratch.at[i], out.at[:, cols], sem.at[i]))
        copies[-1].start()
    for copy in copies:
        copy.wait()


def write_attention(slots, meta, both, *refs):
    q_o, k_o, v_o, o_o, done, scratch, sem = refs[-7:]
    done[...] = jnp.zeros(done.shape, F32)
    rows, c = scratch.shape[1:]
    m = rows // 2

    def copies_of(i, t):
        if t < 3:
            return [pltpu.make_async_copy(scratch.at[i], (q_o, k_o, v_o)[t], sem.at[i, 0])]
        return [
            pltpu.make_async_copy(
                scratch.at[i, pl.ds(j * m, m)], o_o.at[:, pl.ds(j * c, c)], sem.at[i, j]
            )
            for j in range(2)
        ]

    for i, s in enumerate(slots):
        scratch[i] = both[i * rows : (i + 1) * rows].astype(F32)
        for t in range(4):

            @pl.when((meta[0] ^ s) == t)
            def _(i=i, t=t):
                for copy in copies_of(i, t):
                    copy.start()

    for i, s in enumerate(slots):
        for t in range(4):

            @pl.when((meta[0] ^ s) == t)
            def _(i=i, t=t):
                for copy in copies_of(i, t):
                    copy.wait()


class Sum:
    def __init__(self, name, dp, masks, meta, keep=None, send=None):
        self.name, self.dp, self.masks, self.meta = name, dp, masks, meta
        self.keep, self.send, self.small = keep, send, None

    def move(self, a, mask, what):
        pairs = [(2 * i + c, 2 * (i ^ mask[c]) + c) for i in range(self.dp) for c in range(2)]
        with jax.named_scope(f"{self.name}_{what}"):
            return lax.ppermute(a, ("top", "mid", "xy", "seq"), pairs)

    def exchange(self, a, k, what):
        self.got = self.move(a, self.masks[k], what)

    def call(self, body, outs, ins, after, **kw):
        name = f"{self.name}_{body.__name__}" if hasattr(body, "__name__") else f"{self.name}_write"
        return kernel(body, name, outs, ins, after, **{"limit": SUM_LIMIT, **kw})

    def step_a(self):
        self.exchange(self.send, 0, "sum_a")

    def step_b(self, after=(), small=None):
        z, r, c = self.keep.shape[1:]
        ins, self.small = [self.keep, self.got], small
        if small is None:
            self.keep, send = self.call(add_quads, [((z, r, c), BF16)] * 2, ins, after)
        else:
            self.keep, send = self.call(
                self_quads, [((z, r, c), BF16), ((z * r + EXTRA, c), BF16)], [*ins, small], after
            )
        self.exchange(send, 1, "sum_b")
        return self.keep

    def step_c(self, after=()):
        z, r, c = self.keep.shape
        ins, half = [self.keep, self.got], ((2, r, c), BF16)
        if self.small is None:
            self.keep, send = self.call(add_pieces, [half] * 2, ins, after)
        else:
            self.keep, send, self.small = self.call(
                self_pieces,
                [half, ((2 * r + EXTRA, c), BF16), (self.small.shape, BF16)],
                [*ins, self.small],
                after,
            )
        self.exchange(send, 2, "sum_c")
        return self.keep

    def step_d(self, after=()):
        z, r, c = self.keep.shape
        ins, one = [self.keep, self.got], ((r, c), BF16)
        if self.small is None:
            self.keep, send = self.call(add_pair, [one] * 2, ins, after)
        else:
            self.keep, send, self.small = self.call(
                self_pair,
                [one, ((r + EXTRA, c), BF16), (self.small.shape, BF16)],
                [*ins, self.small],
                after,
            )
        self.exchange(send, 3, "sum_d")
        return self.keep

    def step_e(self, after=()):
        ins, one = [self.keep, self.got], (self.keep.shape, BF16)
        if self.small is None:
            self.shard = self.call(add_shard, [one], ins, after)[0]
        else:
            self.shard, self.small = self.call(
                self_shard, [one, (self.small.shape, BF16)], [*ins, self.small], after
            )
        step = 16
        while step < self.dp:
            rest = (step, step)
            self.shard = self.shard + self.move(self.shard, rest, "sum_rest")
            if self.small is not None:
                self.small = self.small + self.move(self.small, rest, "sum_rest")
            step *= 2
        self.exchange(self.shard, 3, "gather_d")
        return self.shard

    def step_f(self, after=()):
        shape = (2,) + self.shard.shape
        self.two = self.call(put_two, [(shape, BF16)], [self.shard, self.got], after)[0]
        self.exchange(self.two, 2, "gather_c")
        return self.two

    def step_g(self, after=()):
        r, c = self.shard.shape
        self.block = self.call(
            join_pieces, [((4 * r, c), BF16)], [self.meta, self.two, self.got], after, smem=1
        )[0]
        self.exchange(self.block, 1, "gather_b")
        return self.block

    def step_h(self, after=()):
        r, c = self.block.shape
        ins = [self.block, self.got]
        if self.small is None:
            self.near = self.call(put_blocks, [((2 * r, c), BF16)], ins, after)[0]
        else:
            self.near = self.call(self_blocks, [((2 * r + EXTRA, c), BF16)], [*ins, self.small], after)[0]
        self.exchange(self.near, 0, "gather_a")
        return self.near

    def write(self, slots, both, into, after):
        body, outs, scratch = self.target
        into = list(into)
        *self.out, done = self.call(
            functools.partial(body, slots),
            [(o, F32) for o in outs] + [((8, 128), F32)],
            [self.meta, both, *into],
            after,
            smem=1,
            in_specs=[VMEM] + [ANY] * len(into),
            out_specs=[ANY] * len(outs) + [VMEM],
            scratch=scratch,
            aliases={2 + i: i for i in range(len(into))},
            limit=30,
            us=2,
        )
        return done

    def write1(self, after=()):
        return self.write((0, 2), self.near, (), after)

    def write2(self, after=()):
        return self.write((1, 3), self.got, self.out, after)


def shards(
    dec_input,
    enc_states,
    dec_lengths,
    enc_lengths,
    rel_buckets,
    out_grad,
    gain_self,
    gain_cross,
    gain_ffn,
    rel_table,
    self_query,
    self_key,
    self_value,
    self_out,
    cross_query,
    cross_key,
    cross_value,
    cross_out,
    ffn_in,
    ffn_out,
    *,
    dp,
):
    docs, size, width = dec_input.shape
    half = enc_states.shape[1]
    rows = docs * size
    n = self_query.shape[1]
    hidden = ffn_in.shape[1]
    block = hidden // 4
    pairs = n // PAIR
    index, core = lax.axis_index(("top", "mid", "xy")), lax.axis_index("seq")
    bits = [(index >> k) & 1 for k in range(4)]
    one, two = jnp.where(core == 0, bits[0], bits[1]), jnp.where(core == 0, bits[1], bits[0])
    near, far, up, top = (1, 2), (2, 1), (4, 4), (8, 8)
    quad, quad_out = one + 2 * two, bits[2] + 2 * one
    meta = jnp.stack([quad, bits[2] + 2 * bits[3], core, quad_out, two + 2 * bits[3]]).astype(jnp.int32)
    meta_out = meta[3:]

    def swap(a):
        return lax.ppermute(a, "seq", [(0, 1), (1, 0)])

    x = dec_input.reshape(rows, width)
    dy = out_grad.reshape(rows, width)
    fo = Sum("ffn_out", dp, (up, near, far, top), meta_out)
    fi = Sum("ffn_in", dp, (near, far, up, top), meta)
    dy_got = fo.move(dy, up, "tokens")
    enc_oth = swap(enc_states)
    self_out_oth, cross_out_oth, cross_query_oth = swap(self_out), swap(cross_out), swap(cross_query)

    tok = (rows, width)
    head = (rows, n)
    h1, q1, k1, v1, o1, lse1 = kernel(
        self_forward,
        "self_forward",
        [(tok, BF16)] + [(head, BF16)] * 4 + [((docs * pairs, 2 * size), F32)],
        [dec_lengths, rel_table.T, *pin(x), gain_self, *pin(self_query, self_key, self_value, rel_buckets)],
        smem=2,
        us=2.7,
    )
    o1_oth = swap(o1)
    kv_shape = (docs, half, 2 * n)
    kv_block = step_block((1, half, 2 * n))
    enc_block = step_block((1, half, width))
    w_block = whole((width, n))
    project = dict(grid=(docs,), in_specs=[enc_block, w_block, w_block], out_specs=[kv_block])
    kv_own = kernel(project_kv, "project_own", [(kv_shape, BF16)], [enc_states, cross_key, cross_value], [o1], us=2, **project)[0]
    kv_oth = kernel(project_kv, "project_oth", [(kv_shape, BF16)], [enc_oth, cross_key, cross_value], [kv_own], us=2, **project)[0]
    wide_tok, wide_head, wo_block = whole(tok), whole(head), whole((n, width))
    gain_block = whole((width,))
    lse_shape = (docs, pairs, 2 * size)
    lse_block = step_block((1, pairs, 2 * size))
    head_block = step_block((size, n))
    x1, h2, q2, o2, lse2 = kernel(
        cross_forward,
        "cross_forward",
        [(tok, F32), (tok, BF16), (head, BF16), (head, BF16), (lse_shape, F32)],
        [meta, enc_lengths, x, o1, o1_oth, self_out, self_out_oth, gain_cross, cross_query, kv_own, kv_oth],
        smem=2,
        grid=(docs,),
        in_specs=[wide_tok, wide_head, wide_head, wo_block, wo_block, gain_block, w_block, kv_block, kv_block],
        out_specs=[wide_tok, wide_tok, wide_head, head_block, lse_block],
        us=8,
    )
    o2_oth = swap(o2)
    group = (2, 4, width // 4, n)
    act = (4, rows, block)
    act_block = pl.BlockSpec((1, rows, block), lambda i, m: (grid_slot(i), 0, 0))
    win_block = pl.BlockSpec((width, block), lambda i, m: (0, m[0] ^ grid_slot(i)))
    wout_block = pl.BlockSpec((block, width), lambda i, m: (m[0] ^ grid_slot(i), 0))
    dz = kernel(
        ffn_act_grad,
        "ffn_act_grad",
        [(act, F32)],
        [meta, dy, ffn_out],
        [o2],
        smem=1,
        grid=(4,),
        in_specs=[wide_tok, wout_block],
        out_specs=[act_block],
        us=2.5,
    )[0]
    pair_act, sent = (2, rows, block), (4, rows, block)
    x2, z_send, z_keep, du_send, du_keep, part = kernel(
        ffn_forward,
        "ffn_forward",
        [(tok, F32), (pair_act, BF16), (pair_act, BF16), (sent, BF16), (pair_act, BF16), (tok, BF16)],
        [meta, x1, o2, o2_oth, cross_out, cross_out_oth, gain_ffn, ffn_in, dz],
        [dy_got],
        smem=1,
        grid=(4,),
        in_specs=[wide_tok, wide_head, wide_head, wo_block, wo_block, gain_block, win_block, act_block],
        out_specs=[wide_tok, whole(pair_act), whole(pair_act), whole(sent), whole(pair_act), wide_tok],
        scratch=[pltpu.VMEM(tok, BF16), pltpu.VMEM(tok, F32)],
        us=8,
    )
    z_got = fo.move(z_send, up, "sum_a")
    du_got = fi.move(du_send, near, "sum_a")
    part_oth = swap(part)
    gain3, dx2, dc, dq2, dkv_own, dkv_oth = kernel(
        cross_backward,
        "cross_backward",
        [((1, width), F32), (tok, F32), (tok, BF16), (head, BF16)] + [(kv_shape, BF16)] * 2,
        [meta, enc_lengths, x2, part, part_oth, gain_ffn, dy, cross_out, q2, lse2, kv_own, kv_oth],
        smem=2,
        grid=(docs,),
        in_specs=[wide_tok, wide_tok, wide_tok, gain_block, wide_tok, wo_block]
        + [head_block, lse_block, kv_block, kv_block],
        out_specs=[whole((1, width)), wide_tok, wide_tok, head_block, kv_block, kv_block],
        scratch=[pltpu.VMEM(head, BF16)],
        us=10,
    )
    dq2_oth = swap(dq2)
    piece = group[1:]
    fo.keep, send = kernel(
        ffn_out_grads, "ffn_out_grads", [(piece, BF16)] * 2, [meta_out, z_keep, z_got, dy, dy_got], [dq2], smem=1, us=3
    )
    fo.exchange(send, 1, "sum_b")
    fi.keep, send = kernel(
        ffn_in_grads, "ffn_in_grads", [(piece, BF16)] * 2, [meta, du_keep, du_send, du_got], [fo.keep], smem=1, us=3
    )
    fi.exchange(send, 1, "sum_b")
    group_scratch = [pltpu.VMEM((4,) + group[1:], BF16), pltpu.SemaphoreType.DMA((4,))]
    enc_rows = (docs * half, width)
    keep, send = kernel(
        cross_grads,
        "cross_grads",
        [(group, BF16)] * 2,
        [meta, h2, dq2, enc_states.reshape(enc_rows), enc_oth.reshape(enc_rows)]
        + [dkv_own.reshape(enc_rows), dkv_oth.reshape(enc_rows), dc, o2],
        [fi.keep],
        smem=1,
        out_specs=[ANY] * 2,
        scratch=group_scratch,
        us=5,
    )
    cross = Sum("cross", dp, (near, far, up, top), meta, keep, send)
    cross.step_a()
    last = fo.step_c([keep])
    last = fi.step_c([last])
    gain2, dx1, da, dqkv, ds1 = kernel(
        self_backward,
        "self_backward",
        [((1, width), F32), (tok, F32), (tok, BF16), ((rows, 3 * n), BF16), ((pairs, docs, size, 2 * size), BF16)],
        [dec_lengths, rel_table.T, x1, dx2, dq2, dq2_oth, cross_query, cross_query_oth, gain_cross, self_out]
        + [q1, k1, v1, lse1, rel_buckets],
        [last],
        smem=2,
        us=5,
    )
    last = ds1
    keep, send = kernel(
        self_grads,
        "self_grads",
        [(group, BF16)] * 2,
        [meta, h1, dqkv, da, o1],
        [last],
        smem=1,
        out_specs=[ANY] * 2,
        scratch=group_scratch,
        us=2.7,
    )
    own = Sum("self", dp, (near, far, up, top), meta, keep, send)
    own.step_a()
    sems = pltpu.SemaphoreType.DMA
    fo.target = (write_ffn_out, [(4, block, width)], [pltpu.VMEM((2, block, width), F32), sems((2,))])
    fi.target = (write_ffn_in, [ffn_in.shape], [pltpu.VMEM((2, width, block), F32), sems((2,))])
    cross.target = own.target = (
        write_attention,
        [(width, n)] * 3 + [(n, width)],
        [pltpu.VMEM((2, width, n), F32), sems((2, 2))],
    )
    last = fo.step_d([keep])
    last = fi.step_d([last])
    last = cross.step_b([last])
    part1 = kernel(
        self_input, "self_input", [(tok, BF16)], [dqkv, self_query, self_key, self_value], [last], us=1
    )[0]
    part1_oth = swap(part1)
    last = fo.step_e([part1])
    last = fi.step_e([last])
    gain1, dx = kernel(
        finish_input,
        "finish_input",
        [((1, width), F32), (tok, F32)],
        [x, part1, part1_oth, gain_self, dx1],
        [last],
        us=2,
    )
    last = dx
    small = kernel(
        small_grads,
        "small_grads",
        [((EXTRA, width // 2), F32)],
        [rel_buckets, ds1, gain1, gain2, gain3],
        [last],
        us=4,
    )[0]
    last = cross.step_c([small])
    last = fo.step_f([last])
    last = fi.step_f([last])
    last = own.step_b([last], small)
    enc_sent = kernel(
        enc_part,
        "enc_part",
        [((docs, half, width), BF16)],
        [dkv_oth, cross_key, cross_value],
        [last],
        grid=(docs,),
        in_specs=[kv_block, w_block, w_block],
        out_specs=[enc_block],
        us=3,
    )[0]
    enc_got = swap(enc_sent)
    last = cross.step_d([enc_sent])
    last = fo.step_g([last])
    last = fi.step_g([last])
    last = own.step_c([last, enc_got])
    last = cross.step_e([last])
    last = fi.step_h([last])
    last = own.step_d([last])
    last = cross.step_f([last])
    last = own.step_e([last])
    last = cross.step_g([last])
    last = own.step_f([last])
    last = fi.write1([last])
    last = cross.step_h([last])
    last = own.step_g([last])
    last = fo.step_h([last])
    enc_grad = kernel(
        finish_enc,
        "finish_enc",
        [((docs, half, width), BF16)],
        [dkv_own, cross_key, cross_value, enc_got],
        [last],
        grid=(docs,),
        in_specs=[kv_block, w_block, w_block, enc_block],
        out_specs=[enc_block],
        us=3,
    )[0]
    last = fi.write2([enc_grad])
    last = own.step_h([last])
    branch = kernel(
        ffn_branch,
        "ffn_branch",
        [(tok, BF16)],
        [meta_out, z_send, z_keep, ffn_out],
        [last],
        smem=1,
        grid=(4,),
        in_specs=[
            pl.BlockSpec((1, rows, block), lambda i, m: (jnp.minimum(i, 1), 0, 0)),
            pl.BlockSpec((1, rows, block), lambda i, m: (jnp.maximum(i - 2, 0), 0, 0)),
            wout_block,
        ],
        out_specs=[wide_tok],
        scratch=[pltpu.VMEM(tok, F32)],
        us=2.5,
    )[0]
    branch_oth = swap(branch)
    last = cross.write1([branch])
    last = fo.write1([last, branch_oth])
    y = kernel(finish_output, "finish_output", [(tok, BF16)], [x2, branch, branch_oth], [last], us=1)[0]
    last = cross.write2([y])
    last = own.write1([last])
    last = fo.write2([last])
    totals = kernel(
        write_small,
        "write_small",
        [((width,), F32)] * 3 + [((n // DH, NB), F32)],
        [own.small, own.got],
        [last],
        limit=16,
    )
    own.write2([totals[-1]])
    return (
        y.reshape(dec_input.shape),
        dx.reshape(dec_input.shape),
        enc_grad,
        totals[0],
        totals[1],
        totals[2],
        totals[3].T,
        *own.out,
        *cross.out,
        fi.out[0],
        fo.out[0].reshape(ffn_out.shape),
    )


def solution(mesh):
    dp = mesh.shape["dp"]
    split = jax.sharding.Mesh(mesh.devices.reshape(dp // 8, 2, 4, 2), ("top", "mid", "xy", "seq"))
    rows = ("top", "mid", "xy")
    col, row, doc = P(None, "seq"), P("seq", None), P(rows, None, None)
    in_specs = (
        (doc, P(rows, "seq", None), P(rows), P(rows), doc, doc)
        + (P(),) * 3
        + (col,) * 4
        + (row,)
        + (col,) * 3
        + (row, col, row)
    )
    out_specs = (
        (doc, doc, P(rows, "seq", None))
        + (P(),) * 3
        + (col,) * 4
        + (row,)
        + (col,) * 3
        + (row, col, row)
    )
    return jax.shard_map(
        functools.partial(shards, dp=dp),
        mesh=split,
        in_specs=in_specs,
        out_specs=out_specs,
        check_vma=False,
    )
```

time: 846 us -> 236 us (0.28)
  waiting for transfers between devices: 511 us -> 63.3 us
  Pallas kernels: 0 us -> 103 us
  blocking collectives: 101 us -> 0 us
  matrix products: 86 us -> 0 us
  local copies, waits for them, and re-layouts: 94.9 us -> 16.8 us
  starting transfers between devices: 0.97 us -> 47.2 us
  other arithmetic: 27.5 us -> 0.07 us
  between operations: 15.3 us -> 1.68 us
    psum x6 -> x0, waiting for transfers between devices: 502 us -> none  [the longest x1 442 us: shards(): lax.psum((gain_self_grad, gain_cross_grad, gain_ffn_grad, table_grad, sel...]
    pallas_call x0 -> x54, Pallas kernels: none -> 103 us  [kernel(): return call(*ins, *after)]
    dot_general x41 -> x0, matrix products: 86 us -> none  [the longest x9 21.8 us: weight_grad(): jnp.einsum('btd,bte->de', left_side, right_side, preferred_element_type=j...]
    psum x1 -> x0, blocking collectives: 80.8 us -> none  [shards(): lax.psum((gain_self_grad, gain_cross_grad, gain_ffn_grad, table_grad, sel...]
    ppermute x0 -> x44, waiting for transfers between devices: none -> 63.3 us  [the longest x33 63.2 us: move(): return lax.ppermute(a, ('top', 'mid', 'xy', 'seq'), pairs)]
    ppermute x0 -> x44, starting transfers between devices: none -> 47.2 us  [the longest x33 45.3 us: move(): return lax.ppermute(a, ('top', 'mid', 'xy', 'seq'), pairs)]
    all_to_all x2 -> x0, blocking collectives: 20.2 us -> none  [the longest x1 13.1 us: shards(): lax.all_to_all(projected, 'seq', split_axis=2, concat_axis=1, tiled=True)]
    unnamed x192 -> x100, local copies, waits for them, and re-layouts: 36.4 us -> 16.7 us
  transfers between devices with their start and end apart: 8 -> 44, of which waited for: 5 -> 16; matrix products, arithmetic and copies ran while one was open for 8% -> 0% of each run, Pallas kernels for 0% -> 39%
where the time goes in v1:
time: 236 us; the launch traced here: 232 us
  Pallas kernels  103 us (44%)
  waiting for transfers between devices  63.3 us (27%)
  starting transfers between devices  47.2 us (20%)
  local copies, waits for them, and re-layouts  16.8 us (7%)
    pallas_call x54, Pallas kernels, kernel(): return call(*ins, *after)  103 us
    ppermute x33, waiting for transfers between devices, move(): return lax.ppermute(a, ('top', 'mid', 'xy', 'seq'), pairs)  63.2 us
    ppermute x33, starting transfers between devices, move(): return lax.ppermute(a, ('top', 'mid', 'xy', 'seq'), pairs)  45.3 us
    unnamed x100, local copies, waits for them, and re-layouts  16.7 us
  transfers between devices with their start and end apart: 44, of which 16 were waited for; matrix products, arithmetic and copies ran while one was open for 0% of the time, Pallas kernels for 39%

profile of v1, /device:TPU:0, one launch (start us, length us, event | category | flops | bytes accessed | tf_op | source)
XLA Modules:
  0.0 232.2 jit_solution(5756526543353694017)
XLA Ops:
  0.7 3.1 %collective-permute-start.5 = (bf16[384,768]{1,0:T(8,128)(2,1)}, bf16[384,768]{1,0:T(8,128)(2,1)}, u32[]{:S(2)}, u32[]{:S(2)}) collective-permute-start(bf16[384,768]{1,0:T(8,128)(2,1)} %bitcast.18), channel_id=1, source_target_pairs={{0,8},{1,9},{2,10},{3,11},{4,12},{5,13},{6,14},{7,15},{8,0},{9,1},... | collective-permute-start | bytes 1769480 | tf_op jit(solution)/shard_map/ffn_out_tokens/ppermute | solution.py:682
  6.3 3.7 %self_forward.1 = (bf16[384,768]{1,0:T(8,128)(2,1)S(1)}, bf16[384,384]{1,0:T(8,128)(2,1)S(1)}, bf16[384,384]{1,0:T(8,128)(2,1)S(1)}, bf16[384,384]{1,0:T(8,128)(...) custom-call(s32[3]{0:T(128)S(1)} %copy-done.30, f32[6,32]{1,0:T(8,128)S(1)} %bitcast.25, ...), custom_call_target="tpu_custom_call" | custom-call | flops 27000000512 | tf_op jit(solution)/shard_map/self_forward/pallas_call | solution.py:78
  15.7 2.1 project_own.1.refs_3_.refs_9_.refs_10_
  17.9 2.1 project_oth.1.refs_10_.refs_11_
  20.1 7.7 %cross_forward.1 = (f32[384,768]{1,0:T(8,128)S(1)}, bf16[384,768]{1,0:T(8,128)(2,1)S(1)}, bf16[384,384]{1,0:T(8,128)(2,1)S(1)}, bf16[384,384]{1,0:T(8,128)(2,1)S(1)}, f32[3,3,256]{2,1,0:T(4,128)S(1)}) custom-call(s32[5]{0:T(128)S(1)} %stack.25.refs_0_, s32[3]{0:T(128)S(1)} %copy-done.29, bf16[384,768]{1,0:T(8,128)(2,1)S(1)} %bitcast.23, ...), custom_call_target="tpu_custom_call" | custom-call | flops 80000000000 | tf_op jit(solution)/shard_map/cross_forward/pallas_call | solution.py:78
  28.0 2.6 %ffn_act_grad.1.refs_8_ = f32[4,384,384]{2,1,0:T(8,128)S(1)} custom-call(s32[5]{0:T(128)S(1)} %stack.25.refs_0_, bf16[384,768]{1,0:T(8,128)(2,1)S(1)} %bitcast.19, bf16[1536,768]{1,0:T(8,128)(2,1)S(1)} %copy-done.1, bf16[384,384]{1,0:T(8,128)(2,1)S(1)} %get-tuple-element.112.refs_3_.refs_2_.refs_8_), custom_call_target="tpu_custom_call" | custom-call | flops 24999999488 | tf_op jit(solution)/shard_map/ffn_act_grad/pallas_call | solution.py:78
  30.6 8.6 %ffn_forward.1 = (f32[384,768]{1,0:T(8,128)S(1)}, bf16[2,384,384]{2,1,0:T(8,128)(2,1)S(1)}, bf16[2,384,384]{2,1,0:T(8,128)(2,1)S(1)}, bf16[4,384,384]{2,1,0:T(8,...) custom-call(s32[5]{0:T(128)S(1)} %stack.25.refs_0_, ...), custom_call_target="tpu_custom_call" | custom-call | flops 80000000000 | tf_op jit(solution)/shard_map/ffn_forward/pallas_call | solution.py:78
  40.1 1.9 collective-permute-start.9
  41.9 9.0 %cross_backward.1 = (f32[1,768]{1,0:T(1,128)S(1)}, f32[384,768]{1,0:T(8,128)S(1)}, bf16[384,768]{1,0:T(8,128)(2,1)S(1)}, bf16[384,384]{1,0:T(8,128)(2,1)S(1)}, b...) custom-call(s32[5]{0:T(128)S(1)} %stack.25.refs_0_, s32[3]{0:T(128)S(1)} %copy-done.29, ...), custom_call_target="tpu_custom_call" | custom-call | flops 99999997952 | tf_op jit(solution)/shard_map/cross_backward/pallas_call | solution.py:78
  51.0 4.6 %collective-permute-done.10.refs_2_ = bf16[2,384,384]{2,1,0:T(8,128)(2,1)S(1)} collective-permute-done((bf16[2,384,384]{2,1,0:T(8,128)(2,1)S(1)}, bf16[2,384,384]{2,1,0:T(8,128)(2,1)S(1)}, u32[]{:S(2)}, u32[]{:S(2)}) %collective-permute-start.10) | collective-permute-done | bytes 589856 | tf_op jit(solution)/shard_map/ffn_out_sum_a/ppermute | solution.py:682
  55.7 2.5 %ffn_out_grads.1 = (bf16[4,192,384]{2,1,0:T(8,128)(2,1)S(1)}, bf16[4,192,384]{2,1,0:T(8,128)(2,1)S(1)}) custom-call(s32[2]{0:T(128)S(1)} %pad_add_fusion.refs_0_, bf16[2,384,384]{2,1,0:T(8,128)(2,1)S(1)} %get-tuple-element.115.refs_1_.refs_2_, bf16[2,384,384]{2,1,0:T(8,128)(2,1)S(1)} %collective-permute-done.10.refs_2_, bf16[384,768]{1,0:T(8,128)(2,1)S(1)} %bitcast.21, ...), custom_call_target="tpu_custom_call" | custom-call | flops 30000001024 | tf_op jit(solution)/shard_map/ffn_out_grads/pallas_call | solution.py:78
  59.7 2.2 ffn_in_grads.1
  63.5 4.6 %cross_grads.1 = (bf16[2,4,192,384]{3,2,1,0:T(8,128)(2,1)S(1)}, bf16[2,4,192,384]{3,2,1,0:T(8,128)(2,1)S(1)}) custom-call(s32[5]{0:T(128)S(1)} %stack.25.refs_0_, bf16[384,768]{1,0:T(8,128)(2,1)S(1)} %get-tuple-element.132.refs_1_, bf16[384,384]{1,0:T(8,128)(2,1)S(1)} %get-tuple-element.121.refs_5_.refs_2_.refs_4_, bf16[984,768]{1,0:T(8,128)(2,1)S(1)} %bitcast.16, ...), custom_call_target="tpu_custom_call" | custom-call | flops 49999998976 | tf_op jit(solution)/shard_map/cross_grads/pallas_call | solution.py:78
  68.7 3.5 %collective-permute-done.12.refs_1_ = bf16[4,192,384]{2,1,0:T(8,128)(2,1)S(1)} collective-permute-done((bf16[4,192,384]{2,1,0:T(8,128)(2,1)S(1)}, bf16[4,192,384]{2,1,0:T(8,128)(2,1)S(1)}, u32[]{:S(2)}, u32[]{:S(2)}) %collective-permute-start.12) | collective-permute-done | bytes 589856 | tf_op jit(solution)/shard_map/ffn_out_sum_b/ppermute | solution.py:682
  72.3 2.7 %collective-permute-start.16 = (bf16[2,192,384]{2,1,0:T(8,128)(2,1)S(1)}, bf16[2,192,384]{2,1,0:T(8,128)(2,1)S(1)}, u32[]{:S(2)}, u32[]{:S(2)}) collective-permute-start(bf16[2,192,384]{2,1,0:T(8,128)(2,1)S(1)} %get-tuple-element.146), channel_id=1, source_target_pairs={{0,4},{1,3},{2,6},{3,1},{4,0},{5,7},{6,2},{7,5},{8,12},{9,11},{10,... | collective-permute-start | bytes 884744 | tf_op jit(solution)/shard_map/ffn_out_sum_c/ppermute | solution.py:682
  78.2 5.6 %self_backward.1 = (f32[1,768]{1,0:T(1,128)S(1)}, f32[384,768]{1,0:T(8,128)S(1)}, bf16[384,768]{1,0:T(8,128)(2,1)S(1)}, bf16[384,1152]{1,0:T(8,128)(2,1)S(1)}, bf16[3,3,128,256]{3,2,1,0:T(8,128)(2,1)S(1)}) custom-call(s32[3]{0:T(128)S(1)} %copy-done.31, f32[6,32]{1,0:T(8,128)S(1)} %bitcast.26, f32[384,768]{1,0:T(8,128)S(1)} %copy-done.43, ...), custom_call_target="tpu_custom_call" | custom-call | flops 49999998976 | tf_op jit(solution)/shard_map/self_backward/pallas_call | solution.py:78
  83.8 12.4 %self_grads.1 = (bf16[2,4,192,384]{3,2,1,0:T(8,128)(2,1)S(1)}, bf16[2,4,192,384]{3,2,1,0:T(8,128)(2,1)S(1)}) custom-call(s32[5]{0:T(128)S(1)} %stack.25.refs_0_, bf16[384,768]{1,0:T(8,128)(2,1)S(1)} %copy-done.41, bf16[384,1152]{1,0:T(8,128)(2,1)S(1)} %get-tuple-element.139.refs_2_.refs_0_, bf16[384,768]{1,0:T(8,128)(2,1)S(1)} %get-tuple-element.140.refs_3_, ...), custom_call_target="tpu_custom_call" | custom-call | flops 27000000512 | tf_op jit(solution)/shard_map/self_grads/pallas_call | solution.py:78
  96.2 2.7 %collective-permute-start.19 = (bf16[192,384]{1,0:T(8,128)(2,1)S(1)}, bf16[192,384]{1,0:T(8,128)(2,1)S(1)}, u32[]{:S(2)}, u32[]{:S(2)}) collective-permute-start(bf16[192,384]{1,0:T(8,128)(2,1)S(1)} %get-tuple-element.152), channel_id=1, source_target_pairs={{0,16},{1,17},{2,18},{3,19},{4,20},{5,21},{6,22},{7,23},{8,24},{9,... | collective-permute-start | bytes 442376 | tf_op jit(solution)/shard_map/ffn_out_sum_d/ppermute | solution.py:682
  98.9 2.4 %collective-permute-start.13 = (bf16[2,4,192,384]{3,2,1,0:T(8,128)(2,1)S(1)}, bf16[2,4,192,384]{3,2,1,0:T(8,128)(2,1)S(1)}, u32[]{:S(2)}, u32[]{:S(2)}) collective-permute-start(bf16[2,4,192,384]{3,2,1,0:T(8,128)(2,1)S(1)} %get-tuple-element.143), channel_id=1, source_target_pairs={{0,2},{1,5},{2,0},{3,7},{4,6},{5,1},{6,4},{7,3},{8,10},{9,13},{10,... | collective-permute-start | bytes 3538952 | tf_op jit(solution)/shard_map/self_sum_a/ppermute | solution.py:682
  104.3 5.3 %collective-permute-done.19.refs_1_ = bf16[192,384]{1,0:T(8,128)(2,1)S(1)} collective-permute-done((bf16[192,384]{1,0:T(8,128)(2,1)S(1)}, bf16[192,384]{1,0:T(8,128)(2,1)S(1)}, u32[]{:S(2)}, u32[]{:S(2)}) %collective-permute-start.19) | collective-permute-done | bytes 147488 | tf_op jit(solution)/shard_map/ffn_out_sum_d/ppermute | solution.py:682
  109.7 4.6 %collective-permute-done.18.refs_1_ = bf16[192,384]{1,0:T(8,128)(2,1)S(1)} collective-permute-done((bf16[192,384]{1,0:T(8,128)(2,1)S(1)}, bf16[192,384]{1,0:T(8,128)(2,1)S(1)}, u32[]{:S(2)}, u32[]{:S(2)}) %collective-permute-start.18) | collective-permute-done | bytes 147488 | tf_op jit(solution)/shard_map/ffn_in_sum_d/ppermute | solution.py:682
  114.4 1.7 collective-permute-start.22
  116.1 1.7 finish_input.1
  119.1 4.3 %small_grads.1.refs_2_ = f32[16,384]{1,0:T(8,128)S(1)} custom-call(s32[3,128,128]{2,1,0:T(8,128)S(1)} %copy-done.21, bf16[3,3,128,256]{3,2,1,0:T(8,128)(2,1)S(1)} %get-tuple-element.141.refs_5_.refs_1_, f32[1,768]{1,0:T(1,128)S(1)} %get-tuple-element.153.refs_2_, f32[1,768]{1,0:T(1,128)S(1)} %get-tuple-element.154.refs_3_, ...), custom_call_target="tpu_custom_call" | custom-call | flops 40000000000 | tf_op jit(solution)/shard_map/small_grads/pallas_call | solution.py:78
  124.4 8.5 %collective-permute-start.26 = (bf16[2,192,384]{2,1,0:T(8,128)(2,1)S(1)}, bf16[2,192,384]{2,1,0:T(8,128)(2,1)S(1)}, u32[]{:S(2)}, u32[]{:S(2)}) collective-permute-start(bf16[2,192,384]{2,1,0:T(8,128)(2,1)S(1)} %get-tuple-element.161), channel_id=1, source_target_pairs={{0,8},{1,9},{2,10},{3,11},{4,12},{5,13},{6,14},{7,15},{8,0},{9,1},... | collective-permute-start | bytes 884744 | tf_op jit(solution)/shard_map/cross_sum_c/ppermute | solution.py:682
  134.3 2.1 enc_part.1.refs_2_
  138.9 4.5 %collective-permute-done.25.refs_2_ = bf16[2,192,384]{2,1,0:T(8,128)(2,1)S(1)} collective-permute-done((bf16[2,192,384]{2,1,0:T(8,128)(2,1)S(1)}, bf16[2,192,384]{2,1,0:T(8,128)(2,1)S(1)}, u32[]{:S(2)}, u32[]{:S(2)}) %collective-permute-start.25) | collective-permute-done | bytes 294944 | tf_op jit(solution)/shard_map/ffn_out_gather_c/ppermute | solution.py:682
  144.0 1.7 collective-permute-start.39
  145.7 3.4 %collective-permute-done.24.refs_2_ = bf16[2,192,384]{2,1,0:T(8,128)(2,1)S(1)} collective-permute-done((bf16[2,192,384]{2,1,0:T(8,128)(2,1)S(1)}, bf16[2,192,384]{2,1,0:T(8,128)(2,1)S(1)}, u32[]{:S(2)}, u32[]{:S(2)}) %collective-permute-start.24) | collective-permute-done | bytes 294944 | tf_op jit(solution)/shard_map/ffn_in_gather_c/ppermute | solution.py:682
  150.7 2.7 %collective-permute-done.23.refs_1_ = bf16[784,384]{1,0:T(8,128)(2,1)S(1)} collective-permute-done((bf16[784,384]{1,0:T(8,128)(2,1)S(1)}, bf16[784,384]{1,0:T(8,128)(2,1)S(1)}, u32[]{:S(2)}, u32[]{:S(2)}) %collective-permute-start.23) | collective-permute-done | bytes 602144 | tf_op jit(solution)/shard_map/self_sum_b/ppermute | solution.py:682
  153.7 2.1 collective-permute-start.28
  155.8 6.6 %collective-permute-done.29.refs_1_ = bf16[768,384]{1,0:T(8,128)(2,1)S(1)} collective-permute-done((bf16[768,384]{1,0:T(8,128)(2,1)S(1)}, bf16[768,384]{1,0:T(8,128)(2,1)S(1)}, u32[]{:S(2)}, u32[]{:S(2)}) %collective-permute-start.29) | collective-permute-done | bytes 589856 | tf_op jit(solution)/shard_map/ffn_in_gather_b/ppermute | solution.py:682
  162.6 1.7 collective-permute-start.38
  164.3 1.7 collective-permute-start.31
  167.7 5.3 %collective-permute-done.31.refs_1_ = bf16[208,384]{1,0:T(8,128)(2,1)S(1)} collective-permute-done((bf16[208,384]{1,0:T(8,128)(2,1)S(1)}, bf16[208,384]{1,0:T(8,128)(2,1)S(1)}, u32[]{:S(2)}, u32[]{:S(2)}) %collective-permute-start.31) | collective-permute-done | bytes 159776 | tf_op jit(solution)/shard_map/self_sum_d/ppermute | solution.py:682
  174.1 3.8 %collective-permute-done.34.refs_2_ = bf16[2,192,384]{2,1,0:T(8,128)(2,1)S(1)} collective-permute-done((bf16[2,192,384]{2,1,0:T(8,128)(2,1)S(1)}, bf16[2,192,384]{2,1,0:T(8,128)(2,1)S(1)}, u32[]{:S(2)}, u32[]{:S(2)}) %collective-permute-start.34) | collective-permute-done | bytes 294944 | tf_op jit(solution)/shard_map/cross_gather_c/ppermute | solution.py:682
  181.4 2.0 ffn_in_write.2
  183.4 5.4 %collective-permute-done.36.refs_1_ = bf16[768,384]{1,0:T(8,128)(2,1)S(1)} collective-permute-done((bf16[768,384]{1,0:T(8,128)(2,1)S(1)}, bf16[768,384]{1,0:T(8,128)(2,1)S(1)}, u32[]{:S(2)}, u32[]{:S(2)}) %collective-permute-start.36) | collective-permute-done | bytes 589856 | tf_op jit(solution)/shard_map/cross_gather_b/ppermute | solution.py:682
  192.5 3.0 %finish_enc.1.refs_3_ = bf16[3,328,768]{2,1,0:T(8,128)(2,1)} custom-call(bf16[3,328,768]{2,1,0:T(8,128)(2,1)S(1)} %get-tuple-element.133.refs_0_, bf16[768,384]{1,0:T(8,128)(2,1)S(1)} %copy-done.15, bf16[768,384]{1,0:T(8,128)(2,1)S(1)} %copy-done.18, bf16[3,328,768]{2,1,0:T(8,128)(2,1)S(1)} %collective-permute-done.27.refs_4_.refs_3_, ...), custom_call_target="tpu_custom_call" | custom-call | flops 30000001024 | tf_op jit(solution)/shard_map/finish_enc/pallas_call | solution.py:78
  196.9 2.0 ffn_in_write.3
  199.0 8.1 %collective-permute-done.37.refs_1_ = bf16[768,384]{1,0:T(8,128)(2,1)S(1)} collective-permute-done((bf16[768,384]{1,0:T(8,128)(2,1)S(1)}, bf16[768,384]{1,0:T(8,128)(2,1)S(1)}, u32[]{:S(2)}, u32[]{:S(2)}) %collective-permute-start.37) | collective-permute-done | bytes 589856 | tf_op jit(solution)/shard_map/self_gather_b/ppermute | solution.py:682
  208.8 2.9 %ffn_branch.1.refs_2_.refs_1_ = bf16[384,768]{1,0:T(8,128)(2,1)S(1)} custom-call(s32[2]{0:T(128)S(1)} %pad_add_fusion.refs_0_, bf16[2,384,384]{2,1,0:T(8,128)(2,1)S(1)} %get-tuple-element.114.refs_1_, bf16[2,384,384]{2,1,0:T(8,128)(2,1)S(1)} %copy-done.39, bf16[1536,768]{1,0:T(8,128)(2,1)S(1)} %copy-done.2, bf16[1552,384]{1,0:T(8,128)(2,1)S(1)} %self_self_blocks.1.refs_4_.refs_1_), custom_call_target="tpu_custom_call" | custom-call | flops 24999999488 | tf_op jit(solution)/shard_map/ffn_branch/pallas_call | solution.py:78
  212.6 2.1 cross_write.2
  214.7 2.9 %ffn_out_write.2 = (f32[4,384,768]{2,1,0:T(8,128)}, f32[8,128]{1,0:T(8,128)S(1)}) custom-call(s32[2]{0:T(128)S(1)} %pad_add_fusion.refs_0_, bf16[1536,384]{1,0:T(8,128)(2,1)} %ffn_out_put_blocks.1.refs_4_.refs_1_, f32[8,128]{1,0:T(8,128)S(1)} %get-tuple-element.175.refs_2_, bf16[384,768]{1,0:T(8,128)(2,1)S(1)} %collective-permute-done.40.refs_3_.refs_2_), custom_call_target="tpu_custom_call" | custom-call | flops 20000000000 | tf_op jit(solution)/shard_map/ffn_out_write/pallas_call | solution.py:78
  219.7 2.0 cross_write.3
  221.7 2.1 self_write.2
  223.8 2.8 %ffn_out_write.3 = (f32[4,384,768]{2,1,0:T(8,128)}, f32[8,128]{1,0:T(8,128)S(1)}) custom-call(s32[2]{0:T(128)S(1)} %pad_add_fusion.refs_0_, bf16[1536,384]{1,0:T(8,128)(2,1)} %collective-permute-done.42.refs_1_, f32[4,384,768]{2,1,0:T(8,128)} %get-tuple-element.177.refs_2_, f32[8,128]{1,0:T(8,128)S(1)} %get-tuple-element.183.refs_3_), custom_call_target="tpu_custom_call", output_to_operand_aliasing={{0}: (2, {})} | custom-call | flops 20000000000 | tf_op jit(solution)/shard_map/ffn_out_write/pallas_call | solution.py:78
  229.3 2.6 %self_write.3 = (f32[768,384]{1,0:T(8,128)}, f32[768,384]{1,0:T(8,128)}, f32[768,384]{1,0:T(8,128)}, f32[384,768]{1,0:T(8,128)}, f32[8,128]{1,0:T(8,128)}) custom-call(s32[5]{0:T(128)S(1)} %stack.25.refs_0_, bf16[1552,384]{1,0:T(8,128)(2,1)S(1)} %collective-permute-done.41.refs_1_, ...), custom_call_target="tpu_custom_call", output_to_operand_aliasing={{0}: (2, {}), {1}: (3, {}), {2}: (4, {}), {3}: (5, {})} | custom-call | flops 20000000000 | tf_op jit(solution)/shard_map/self_write/pallas_call | solution.py:78
  (196 shorter events, 47.3 us)
Async XLA Ops:
  0.7 29.9 %collective-permute-start.5 = (bf16[384,768]{1,0:T(8,128)(2,1)}, bf16[384,768]{1,0:T(8,128)(2,1)}, u32[]{:S(2)}, u32[]{:S(2)}) collective-permute-start(bf16[384,768]{1,0:T(8,128)(2,1)} %bitcast.18), channel_id=1, source_target_pairs={{0,8},{1,9},{2,10},{3,11},{4,12},{5,13},{6,14},{7,15},{8,0},{9,1},... | collective-permute-start | bytes 1769480 | tf_op jit(solution)/shard_map/ffn_out_tokens/ppermute | solution.py:682
  3.7 16.3 %collective-permute-start.1 = (bf16[384,768]{1,0:T(8,128)(2,1)}, bf16[384,768]{1,0:T(8,128)(2,1)}, u32[]{:S(2)}, u32[]{:S(2)}) collective-permute-start(bf16[384,768]{1,0:T(8,128)(2,1)} %refs_9_.1), channel_id=1, source_target_pairs={{0,1},{1,0},{2,3},{3,2},{4,5},{5,4},{6,7},{7,6},{8,9},{9,8},{10,11... | collective-permute-start | bytes 1769480 | tf_op jit(solution)/shard_map/ppermute | solution.py:843
  3.7 26.8 %collective-permute-start.4 = (bf16[384,768]{1,0:T(8,128)(2,1)}, bf16[384,768]{1,0:T(8,128)(2,1)}, u32[]{:S(2)}, u32[]{:S(2)}) collective-permute-start(bf16[384,768]{1,0:T(8,128)(2,1)} %refs_7_.7), channel_id=1, source_target_pairs={{0,1},{1,0},{2,3},{3,2},{4,5},{5,4},{6,7},{7,6},{8,9},{9,8},{10,11... | collective-permute-start | bytes 1769480 | tf_op jit(solution)/shard_map/ppermute | solution.py:843
  4.3 13.6 %collective-permute-start.2 = (bf16[3,328,768]{2,1,0:T(8,128)(2,1)}, bf16[3,328,768]{2,1,0:T(8,128)(2,1)S(1)}, u32[]{:S(2)}, u32[]{:S(2)}) collective-permute-start(bf16[3,328,768]{2,1,0:T(8,128)(2,1)} %refs_0_.5), channel_id=1, source_target_pairs={{0,1},{1,0},{2,3},{3,2},{4,5},{5,4},{6,7},{7,6},{8,9},{9,8},{10,11... | collective-permute-start | bytes 4534280 | tf_op jit(solution)/shard_map/ppermute | solution.py:843
  12.9 7.1 %collective-permute-start = (bf16[384,384]{1,0:T(8,128)(2,1)S(1)}, bf16[384,384]{1,0:T(8,128)(2,1)}, u32[]{:S(2)}, u32[]{:S(2)}) collective-permute-start(bf16[384,384]{1,0:T(8,128)(2,1)S(1)} %get-tuple-element.110.refs_3_.refs_4_), channel_id=1, source_target_pairs={{0,1},{1,0},{2,3},{3,2},{4,5},{5,4},{6,7},{7,6},{8,9},{9,8},{10,11... | collective-permute-start | bytes 884744 | tf_op jit(solution)/shard_map/ppermute | solution.py:843
  20.0 8.0 %copy-start.1 = (bf16[1536,768]{1,0:T(8,128)(2,1)S(1)}, bf16[1536,768]{1,0:T(8,128)(2,1)}, u32[]{:S(2)}) copy-start(bf16[1536,768]{1,0:T(8,128)(2,1)} %refs_3_.7) | copy-start | bytes 7077892
  20.0 8.0 %copy-start.5 = (bf16[3,128,768]{2,1,0:T(8,128)(2,1)S(1)}, bf16[3,128,768]{2,1,0:T(8,128)(2,1)}, u32[]{:S(2)}) copy-start(bf16[3,128,768]{2,1,0:T(8,128)(2,1)} %param.25) | copy-start | bytes 1769476
  27.9 2.7 %collective-permute-start.3 = (bf16[384,384]{1,0:T(8,128)(2,1)S(1)}, bf16[384,384]{1,0:T(8,128)(2,1)S(1)}, u32[]{:S(2)}, u32[]{:S(2)}) collective-permute-start(bf16[384,384]{1,0:T(8,128)(2,1)S(1)} %get-tuple-element.112.refs_3_.refs_2_.refs_8_), channel_id=1, source_target_pairs={{0,1},{1,0},{2,3},{3,2},{4,5},{5,4},{6,7},{7,6},{8,9},{9,8},{10,11... | collective-permute-start | bytes 884744 | tf_op jit(solution)/shard_map/ppermute | solution.py:843
  39.2 11.7 %copy-start.36 = (f32[384,768]{1,0:T(8,128)}, f32[384,768]{1,0:T(8,128)S(1)}, u32[]{:S(2)}) copy-start(f32[384,768]{1,0:T(8,128)S(1)} %get-tuple-element.113.refs_2_.refs_0_) | copy-start | bytes 3538948
  39.3 16.4 %copy-start.38 = (bf16[2,384,384]{2,1,0:T(8,128)(2,1)}, bf16[2,384,384]{2,1,0:T(8,128)(2,1)S(1)}, u32[]{:S(2)}) copy-start(bf16[2,384,384]{2,1,0:T(8,128)(2,1)S(1)} %get-tuple-element.115.refs_1_.refs_2_) | copy-start | bytes 1769476
  39.3 2.7 %collective-permute-start.6 = (bf16[384,768]{1,0:T(8,128)(2,1)S(1)}, bf16[384,768]{1,0:T(8,128)(2,1)S(1)}, u32[]{:S(2)}, u32[]{:S(2)}) collective-permute-start(bf16[384,768]{1,0:T(8,128)(2,1)S(1)} %get-tuple-element.117.refs_3_), channel_id=1, source_target_pairs={{0,1},{1,0},{2,3},{3,2},{4,5},{5,4},{6,7},{7,6},{8,9},{9,8},{10,11... | collective-permute-start | bytes 1769480 | tf_op jit(solution)/shard_map/ppermute | solution.py:843
  39.8 37.2 %collective-permute-start.8 = (bf16[768,384]{1,0:T(8,128)(2,1)}, bf16[768,384]{1,0:T(8,128)(2,1)}, u32[]{:S(2)}, u32[]{:S(2)}) collective-permute-start(bf16[768,384]{1,0:T(8,128)(2,1)} %refs_6_.5), channel_id=1, source_target_pairs={{0,1},{1,0},{2,3},{3,2},{4,5},{5,4},{6,7},{7,6},{8,9},{9,8},{10,11... | collective-permute-start | bytes 1769480 | tf_op jit(solution)/shard_map/ppermute | solution.py:843
  40.0 15.7 %collective-permute-start.10 = (bf16[2,384,384]{2,1,0:T(8,128)(2,1)S(1)}, bf16[2,384,384]{2,1,0:T(8,128)(2,1)S(1)}, u32[]{:S(2)}, u32[]{:S(2)}) collective-permute-start(bf16[2,384,384]{2,1,0:T(8,128)(2,1)S(1)} %get-tuple-element.114.refs_1_), channel_id=1, source_target_pairs={{0,8},{1,9},{2,10},{3,11},{4,12},{5,13},{6,14},{7,15},{8,0},{9,1},... | collective-permute-start | bytes 1769480 | tf_op jit(solution)/shard_map/ffn_out_sum_a/ppermute | solution.py:682
  40.1 19.7 %collective-permute-start.9 = (bf16[4,384,384]{2,1,0:T(8,128)(2,1)S(1)}, bf16[4,384,384]{2,1,0:T(8,128)(2,1)S(1)}, u32[]{:S(2)}, u32[]{:S(2)}) collective-permute-start(bf16[4,384,384]{2,1,0:T(8,128)(2,1)S(1)} %get-tuple-element.127.refs_2_), channel_id=1, source_target_pairs={{0,2},{1,5},{2,0},{3,7},{4,6},{5,1},{6,4},{7,3},{8,10},{9,13},{10,... | collective-permute-start | bytes 3538952 | tf_op jit(solution)/shard_map/ffn_in_sum_a/ppermute | solution.py:682
  50.9 26.1 %collective-permute-start.7 = (bf16[384,384]{1,0:T(8,128)(2,1)S(1)}, bf16[384,384]{1,0:T(8,128)(2,1)S(1)}, u32[]{:S(2)}, u32[]{:S(2)}) collective-permute-start(bf16[384,384]{1,0:T(8,128)(2,1)S(1)} %get-tuple-element.121.refs_5_.refs_2_.refs_4_), channel_id=1, source_target_pairs={{0,1},{1,0},{2,3},{3,2},{4,5},{5,4},{6,7},{7,6},{8,9},{9,8},{10,11... | collective-permute-start | bytes 884744 | tf_op jit(solution)/shard_map/ppermute | solution.py:843
  58.2 14.0 %collective-permute-start.12 = (bf16[4,192,384]{2,1,0:T(8,128)(2,1)S(1)}, bf16[4,192,384]{2,1,0:T(8,128)(2,1)S(1)}, u32[]{:S(2)}, u32[]{:S(2)}) collective-permute-start(bf16[4,192,384]{2,1,0:T(8,128)(2,1)S(1)} %get-tuple-element.131), channel_id=1, source_target_pairs={{0,2},{1,5},{2,0},{3,7},{4,6},{5,1},{6,4},{7,3},{8,10},{9,13},{10,... | collective-permute-start | bytes 1769480 | tf_op jit(solution)/shard_map/ffn_out_sum_b/ppermute | solution.py:682
  61.9 14.5 %collective-permute-start.11 = (bf16[4,192,384]{2,1,0:T(8,128)(2,1)S(1)}, bf16[4,192,384]{2,1,0:T(8,128)(2,1)S(1)}, u32[]{:S(2)}, u32[]{:S(2)}) collective-permute-start(bf16[4,192,384]{2,1,0:T(8,128)(2,1)S(1)} %get-tuple-element.130), channel_id=1, source_target_pairs={{0,4},{1,3},{2,6},{3,1},{4,0},{5,7},{6,2},{7,5},{8,12},{9,11},{10,... | collective-permute-start | bytes 1769480 | tf_op jit(solution)/shard_map/ffn_in_sum_b/ppermute | solution.py:682
  68.1 33.6 %collective-permute-start.14 = (bf16[2,4,192,384]{3,2,1,0:T(8,128)(2,1)S(1)}, bf16[2,4,192,384]{3,2,1,0:T(8,128)(2,1)S(1)}, u32[]{:S(2)}, u32[]{:S(2)}) collective-permute-start(bf16[2,4,192,384]{3,2,1,0:T(8,128)(2,1)S(1)} %get-tuple-element.144), channel_id=1, source_target_pairs={{0,2},{1,5},{2,0},{3,7},{4,6},{5,1},{6,4},{7,3},{8,10},{9,13},{10,... | collective-permute-start | bytes 3538952 | tf_op jit(solution)/shard_map/cross_sum_a/ppermute | solution.py:682
  72.3 23.9 %collective-permute-start.16 = (bf16[2,192,384]{2,1,0:T(8,128)(2,1)S(1)}, bf16[2,192,384]{2,1,0:T(8,128)(2,1)S(1)}, u32[]{:S(2)}, u32[]{:S(2)}) collective-permute-start(bf16[2,192,384]{2,1,0:T(8,128)(2,1)S(1)} %get-tuple-element.146), channel_id=1, source_target_pairs={{0,4},{1,3},{2,6},{3,1},{4,0},{5,7},{6,2},{7,5},{8,12},{9,11},{10,... | collective-permute-start | bytes 884744 | tf_op jit(solution)/shard_map/ffn_out_sum_c/ppermute | solution.py:682
  76.5 24.7 %collective-permute-start.15 = (bf16[2,192,384]{2,1,0:T(8,128)(2,1)S(1)}, bf16[2,192,384]{2,1,0:T(8,128)(2,1)S(1)}, u32[]{:S(2)}, u32[]{:S(2)}) collective-permute-start(bf16[2,192,384]{2,1,0:T(8,128)(2,1)S(1)} %get-tuple-element.145), channel_id=1, source_target_pairs={{0,8},{1,9},{2,10},{3,11},{4,12},{5,13},{6,14},{7,15},{8,0},{9,1},... | collective-permute-start | bytes 884744 | tf_op jit(solution)/shard_map/ffn_in_sum_c/ppermute | solution.py:682
  96.2 13.4 %collective-permute-start.19 = (bf16[192,384]{1,0:T(8,128)(2,1)S(1)}, bf16[192,384]{1,0:T(8,128)(2,1)S(1)}, u32[]{:S(2)}, u32[]{:S(2)}) collective-permute-start(bf16[192,384]{1,0:T(8,128)(2,1)S(1)} %get-tuple-element.152), channel_id=1, source_target_pairs={{0,16},{1,17},{2,18},{3,19},{4,20},{5,21},{6,22},{7,23},{8,24},{9,... | collective-permute-start | bytes 442376 | tf_op jit(solution)/shard_map/ffn_out_sum_d/ppermute | solution.py:682
  98.9 34.2 %collective-permute-start.13 = (bf16[2,4,192,384]{3,2,1,0:T(8,128)(2,1)S(1)}, bf16[2,4,192,384]{3,2,1,0:T(8,128)(2,1)S(1)}, u32[]{:S(2)}, u32[]{:S(2)}) collective-permute-start(bf16[2,4,192,384]{3,2,1,0:T(8,128)(2,1)S(1)} %get-tuple-element.143), channel_id=1, source_target_pairs={{0,2},{1,5},{2,0},{3,7},{4,6},{5,1},{6,4},{7,3},{8,10},{9,13},{10,... | collective-permute-start | bytes 3538952 | tf_op jit(solution)/shard_map/self_sum_a/ppermute | solution.py:682
  101.3 13.0 %collective-permute-start.18 = (bf16[192,384]{1,0:T(8,128)(2,1)S(1)}, bf16[192,384]{1,0:T(8,128)(2,1)S(1)}, u32[]{:S(2)}, u32[]{:S(2)}) collective-permute-start(bf16[192,384]{1,0:T(8,128)(2,1)S(1)} %get-tuple-element.151), channel_id=1, source_target_pairs={{0,16},{1,17},{2,18},{3,19},{4,20},{5,21},{6,22},{7,23},{8,24},{9,... | collective-permute-start | bytes 442376 | tf_op jit(solution)/shard_map/ffn_in_sum_d/ppermute | solution.py:682
  104.2 11.9 %collective-permute-start.17 = (bf16[384,768]{1,0:T(8,128)(2,1)S(1)}, bf16[384,768]{1,0:T(8,128)(2,1)S(1)}, u32[]{:S(2)}, u32[]{:S(2)}) collective-permute-start(bf16[384,768]{1,0:T(8,128)(2,1)S(1)} %self_input.1.refs_2_.refs_1_), channel_id=1, source_target_pairs={{0,1},{1,0},{2,3},{3,2},{4,5},{5,4},{6,7},{7,6},{8,9},{9,8},{10,11... | collective-permute-start | bytes 1769480 | tf_op jit(solution)/shard_map/ppermute | solution.py:843
  109.6 23.3 %collective-permute-start.21 = (bf16[192,384]{1,0:T(8,128)(2,1)S(1)}, bf16[192,384]{1,0:T(8,128)(2,1)S(1)}, u32[]{:S(2)}, u32[]{:S(2)}) collective-permute-start(bf16[192,384]{1,0:T(8,128)(2,1)S(1)} %ffn_out_add_shard.1.refs_2_.refs_0_), channel_id=1, source_target_pairs={{0,16},{1,17},{2,18},{3,19},{4,20},{5,21},{6,22},{7,23},{8,24},{9,... | collective-permute-start | bytes 442376 | tf_op jit(solution)/shard_map/ffn_out_gather_d/ppermute | solution.py:682
  114.3 18.7 %collective-permute-start.20 = (bf16[192,384]{1,0:T(8,128)(2,1)S(1)}, bf16[192,384]{1,0:T(8,128)(2,1)S(1)}, u32[]{:S(2)}, u32[]{:S(2)}) collective-permute-start(bf16[192,384]{1,0:T(8,128)(2,1)S(1)} %ffn_in_add_shard.1.refs_5_.refs_0_), channel_id=1, source_target_pairs={{0,16},{1,17},{2,18},{3,19},{4,20},{5,21},{6,22},{7,23},{8,24},{9,... | collective-permute-start | bytes 442376 | tf_op jit(solution)/shard_map/ffn_in_gather_d/ppermute | solution.py:682
  114.4 9.9 %collective-permute-start.22 = (bf16[4,192,384]{2,1,0:T(8,128)(2,1)S(1)}, bf16[4,192,384]{2,1,0:T(8,128)(2,1)S(1)}, u32[]{:S(2)}, u32[]{:S(2)}) collective-permute-start(bf16[4,192,384]{2,1,0:T(8,128)(2,1)S(1)} %get-tuple-element.157), channel_id=1, source_target_pairs={{0,4},{1,3},{2,6},{3,1},{4,0},{5,7},{6,2},{7,5},{8,12},{9,11},{10,... | collective-permute-start | bytes 1769480 | tf_op jit(solution)/shard_map/cross_sum_b/ppermute | solution.py:682
  124.4 14.2 %collective-permute-start.26 = (bf16[2,192,384]{2,1,0:T(8,128)(2,1)S(1)}, bf16[2,192,384]{2,1,0:T(8,128)(2,1)S(1)}, u32[]{:S(2)}, u32[]{:S(2)}) collective-permute-start(bf16[2,192,384]{2,1,0:T(8,128)(2,1)S(1)} %get-tuple-element.161), channel_id=1, source_target_pairs={{0,8},{1,9},{2,10},{3,11},{4,12},{5,13},{6,14},{7,15},{8,0},{9,1},... | collective-permute-start | bytes 884744 | tf_op jit(solution)/shard_map/cross_sum_c/ppermute | solution.py:682
  136.4 17.0 %collective-permute-start.27 = (bf16[3,328,768]{2,1,0:T(8,128)(2,1)S(1)}, bf16[3,328,768]{2,1,0:T(8,128)(2,1)S(1)}, u32[]{:S(2)}, u32[]{:S(2)}) collective-permute-start(bf16[3,328,768]{2,1,0:T(8,128)(2,1)S(1)} %enc_part.1.refs_2_), channel_id=1, source_target_pairs={{0,1},{1,0},{2,3},{3,2},{4,5},{5,4},{6,7},{7,6},{8,9},{9,8},{10,11... | collective-permute-start | bytes 4534280 | tf_op jit(solution)/shard_map/ppermute | solution.py:843
  136.5 12.6 %collective-permute-start.24 = (bf16[2,192,384]{2,1,0:T(8,128)(2,1)S(1)}, bf16[2,192,384]{2,1,0:T(8,128)(2,1)S(1)}, u32[]{:S(2)}, u32[]{:S(2)}) collective-permute-start(bf16[2,192,384]{2,1,0:T(8,128)(2,1)S(1)} %ffn_in_put_two.1.refs_3_.refs_1_), channel_id=1, source_target_pairs={{0,8},{1,9},{2,10},{3,11},{4,12},{5,13},{6,14},{7,15},{8,0},{9,1},... | collective-permute-start | bytes 884744 | tf_op jit(solution)/shard_map/ffn_in_gather_c/ppermute | solution.py:682
  136.6 6.8 %collective-permute-start.25 = (bf16[2,192,384]{2,1,0:T(8,128)(2,1)S(1)}, bf16[2,192,384]{2,1,0:T(8,128)(2,1)S(1)}, u32[]{:S(2)}, u32[]{:S(2)}) collective-permute-start(bf16[2,192,384]{2,1,0:T(8,128)(2,1)S(1)} %ffn_out_put_two.1.refs_2_.refs_1_), channel_id=1, source_target_pairs={{0,4},{1,3},{2,6},{3,1},{4,0},{5,7},{6,2},{7,5},{8,12},{9,11},{10,... | collective-permute-start | bytes 884744 | tf_op jit(solution)/shard_map/ffn_out_gather_c/ppermute | solution.py:682
  137.6 15.8 %collective-permute-start.23 = (bf16[784,384]{1,0:T(8,128)(2,1)S(1)}, bf16[784,384]{1,0:T(8,128)(2,1)S(1)}, u32[]{:S(2)}, u32[]{:S(2)}) collective-permute-start(bf16[784,384]{1,0:T(8,128)(2,1)S(1)} %get-tuple-element.160), channel_id=1, source_target_pairs={{0,4},{1,3},{2,6},{3,1},{4,0},{5,7},{6,2},{7,5},{8,12},{9,11},{10,... | collective-permute-start | bytes 1806344 | tf_op jit(solution)/shard_map/self_sum_b/ppermute | solution.py:682
  138.7 14.8 %collective-permute-start.30 = (bf16[192,384]{1,0:T(8,128)(2,1)S(1)}, bf16[192,384]{1,0:T(8,128)(2,1)S(1)}, u32[]{:S(2)}, u32[]{:S(2)}) collective-permute-start(bf16[192,384]{1,0:T(8,128)(2,1)S(1)} %get-tuple-element.166), channel_id=1, source_target_pairs={{0,16},{1,17},{2,18},{3,19},{4,20},{5,21},{6,22},{7,23},{8,24},{9,... | collective-permute-start | bytes 442376 | tf_op jit(solution)/shard_map/cross_sum_d/ppermute | solution.py:682
  144.0 47.4 %collective-permute-start.39 = (bf16[768,384]{1,0:T(8,128)(2,1)S(1)}, bf16[768,384]{1,0:T(8,128)(2,1)S(1)}, u32[]{:S(2)}, u32[]{:S(2)}) collective-permute-start(bf16[768,384]{1,0:T(8,128)(2,1)S(1)} %ffn_out_join_pieces.1.refs_3_.refs_0_), channel_id=1, source_target_pairs={{0,2},{1,5},{2,0},{3,7},{4,6},{5,1},{6,4},{7,3},{8,10},{9,13},{10,... | collective-permute-start | bytes 1769480 | tf_op jit(solution)/shard_map/ffn_out_gather_b/ppermute | solution.py:682
  149.7 12.8 %collective-permute-start.29 = (bf16[768,384]{1,0:T(8,128)(2,1)S(1)}, bf16[768,384]{1,0:T(8,128)(2,1)S(1)}, u32[]{:S(2)}, u32[]{:S(2)}) collective-permute-start(bf16[768,384]{1,0:T(8,128)(2,1)S(1)} %ffn_in_join_pieces.1.refs_3_.refs_0_), channel_id=1, source_target_pairs={{0,4},{1,3},{2,6},{3,1},{4,0},{5,7},{6,2},{7,5},{8,12},{9,11},{10,... | collective-permute-start | bytes 1769480 | tf_op jit(solution)/shard_map/ffn_in_gather_b/ppermute | solution.py:682
  153.6 12.4 %collective-permute-start.32 = (bf16[192,384]{1,0:T(8,128)(2,1)S(1)}, bf16[192,384]{1,0:T(8,128)(2,1)S(1)}, u32[]{:S(2)}, u32[]{:S(2)}) collective-permute-start(bf16[192,384]{1,0:T(8,128)(2,1)S(1)} %cross_add_shard.1.refs_2_.refs_0_), channel_id=1, source_target_pairs={{0,16},{1,17},{2,18},{3,19},{4,20},{5,21},{6,22},{7,23},{8,24},{9,... | collective-permute-start | bytes 442376 | tf_op jit(solution)/shard_map/cross_gather_d/ppermute | solution.py:682
  153.7 10.5 %collective-permute-start.28 = (bf16[400,384]{1,0:T(8,128)(2,1)S(1)}, bf16[400,384]{1,0:T(8,128)(2,1)S(1)}, u32[]{:S(2)}, u32[]{:S(2)}) collective-permute-start(bf16[400,384]{1,0:T(8,128)(2,1)S(1)} %get-tuple-element.164), channel_id=1, source_target_pairs={{0,8},{1,9},{2,10},{3,11},{4,12},{5,13},{6,14},{7,15},{8,0},{9,1},... | collective-permute-start | bytes 921608 | tf_op jit(solution)/shard_map/self_sum_c/ppermute | solution.py:682
  162.6 33.0 %collective-permute-start.38 = (bf16[1536,384]{1,0:T(8,128)(2,1)S(1)}, bf16[1536,384]{1,0:T(8,128)(2,1)S(1)}, u32[]{:S(2)}, u32[]{:S(2)}) collective-permute-start(bf16[1536,384]{1,0:T(8,128)(2,1)S(1)} %ffn_in_put_blocks.1.refs_3_.refs_1_), channel_id=1, source_target_pairs={{0,2},{1,5},{2,0},{3,7},{4,6},{5,1},{6,4},{7,3},{8,10},{9,13},{10,... | collective-permute-start | bytes 3538952 | tf_op jit(solution)/shard_map/ffn_in_gather_a/ppermute | solution.py:682
  164.3 8.7 %collective-permute-start.31 = (bf16[208,384]{1,0:T(8,128)(2,1)S(1)}, bf16[208,384]{1,0:T(8,128)(2,1)S(1)}, u32[]{:S(2)}, u32[]{:S(2)}) collective-permute-start(bf16[208,384]{1,0:T(8,128)(2,1)S(1)} %get-tuple-element.168), channel_id=1, source_target_pairs={{0,16},{1,17},{2,18},{3,19},{4,20},{5,21},{6,22},{7,23},{8,24},{9,... | collective-permute-start | bytes 479240 | tf_op jit(solution)/shard_map/self_sum_d/ppermute | solution.py:682
  166.0 11.8 %collective-permute-start.34 = (bf16[2,192,384]{2,1,0:T(8,128)(2,1)S(1)}, bf16[2,192,384]{2,1,0:T(8,128)(2,1)S(1)}, u32[]{:S(2)}, u32[]{:S(2)}) collective-permute-start(bf16[2,192,384]{2,1,0:T(8,128)(2,1)S(1)} %cross_put_two.1.refs_3_.refs_1_), channel_id=1, source_target_pairs={{0,8},{1,9},{2,10},{3,11},{4,12},{5,13},{6,14},{7,15},{8,0},{9,1},... | collective-permute-start | bytes 884744 | tf_op jit(solution)/shard_map/cross_gather_c/ppermute | solution.py:682
  173.0 8.0 %collective-permute-start.33 = (bf16[192,384]{1,0:T(8,128)(2,1)S(1)}, bf16[192,384]{1,0:T(8,128)(2,1)S(1)}, u32[]{:S(2)}, u32[]{:S(2)}) collective-permute-start(bf16[192,384]{1,0:T(8,128)(2,1)S(1)} %get-tuple-element.170.refs_3_.refs_0_), channel_id=1, source_target_pairs={{0,16},{1,17},{2,18},{3,19},{4,20},{5,21},{6,22},{7,23},{8,24},{9,... | collective-permute-start | bytes 442376 | tf_op jit(solution)/shard_map/self_gather_d/ppermute | solution.py:682
  178.5 10.3 %collective-permute-start.36 = (bf16[768,384]{1,0:T(8,128)(2,1)S(1)}, bf16[768,384]{1,0:T(8,128)(2,1)S(1)}, u32[]{:S(2)}, u32[]{:S(2)}) collective-permute-start(bf16[768,384]{1,0:T(8,128)(2,1)S(1)} %cross_join_pieces.1.refs_2_.refs_0_), channel_id=1, source_target_pairs={{0,4},{1,3},{2,6},{3,1},{4,0},{5,7},{6,2},{7,5},{8,12},{9,11},{10,... | collective-permute-start | bytes 1769480 | tf_op jit(solution)/shard_map/cross_gather_b/ppermute | solution.py:682
  181.1 9.0 %collective-permute-start.35 = (bf16[2,192,384]{2,1,0:T(8,128)(2,1)S(1)}, bf16[2,192,384]{2,1,0:T(8,128)(2,1)S(1)}, u32[]{:S(2)}, u32[]{:S(2)}) collective-permute-start(bf16[2,192,384]{2,1,0:T(8,128)(2,1)S(1)} %self_put_two.1.refs_2_.refs_1_), channel_id=1, source_target_pairs={{0,8},{1,9},{2,10},{3,11},{4,12},{5,13},{6,14},{7,15},{8,0},{9,1},... | collective-permute-start | bytes 884744 | tf_op jit(solution)/shard_map/self_gather_c/ppermute | solution.py:682
  188.9 29.7 %collective-permute-start.43 = (bf16[1536,384]{1,0:T(8,128)(2,1)S(1)}, bf16[1536,384]{1,0:T(8,128)(2,1)S(1)}, u32[]{:S(2)}, u32[]{:S(2)}) collective-permute-start(bf16[1536,384]{1,0:T(8,128)(2,1)S(1)} %cross_put_blocks.1.refs_3_.refs_1_), channel_id=1, source_target_pairs={{0,2},{1,5},{2,0},{3,7},{4,6},{5,1},{6,4},{7,3},{8,10},{9,13},{10,... | collective-permute-start | bytes 3538952 | tf_op jit(solution)/shard_map/cross_gather_a/ppermute | solution.py:682
  190.7 16.3 %collective-permute-start.37 = (bf16[768,384]{1,0:T(8,128)(2,1)S(1)}, bf16[768,384]{1,0:T(8,128)(2,1)S(1)}, u32[]{:S(2)}, u32[]{:S(2)}) collective-permute-start(bf16[768,384]{1,0:T(8,128)(2,1)S(1)} %self_join_pieces.1.refs_2_.refs_0_), channel_id=1, source_target_pairs={{0,4},{1,3},{2,6},{3,1},{4,0},{5,7},{6,2},{7,5},{8,12},{9,11},{10,... | collective-permute-start | bytes 1769480 | tf_op jit(solution)/shard_map/self_gather_b/ppermute | solution.py:682
  192.5 31.3 %collective-permute-start.42 = (bf16[1536,384]{1,0:T(8,128)(2,1)}, bf16[1536,384]{1,0:T(8,128)(2,1)}, u32[]{:S(2)}, u32[]{:S(2)}) collective-permute-start(bf16[1536,384]{1,0:T(8,128)(2,1)} %ffn_out_put_blocks.1.refs_4_.refs_1_), channel_id=1, source_target_pairs={{0,8},{1,9},{2,10},{3,11},{4,12},{5,13},{6,14},{7,15},{8,0},{9,1},... | collective-permute-start | bytes 3538952 | tf_op jit(solution)/shard_map/ffn_out_gather_a/ppermute | solution.py:682
  211.7 16.4 %collective-permute-start.41 = (bf16[1552,384]{1,0:T(8,128)(2,1)S(1)}, bf16[1552,384]{1,0:T(8,128)(2,1)S(1)}, u32[]{:S(2)}, u32[]{:S(2)}) collective-permute-start(bf16[1552,384]{1,0:T(8,128)(2,1)S(1)} %self_self_blocks.1.refs_4_.refs_1_), channel_id=1, source_target_pairs={{0,2},{1,5},{2,0},{3,7},{4,6},{5,1},{6,4},{7,3},{8,10},{9,13},{10,... | collective-permute-start | bytes 3575816 | tf_op jit(solution)/shard_map/self_gather_a/ppermute | solution.py:682
  212.6 2.1 collective-permute-start.40
  (46 other events, 92.7 us)
